TPU v7x, 1024 devices: a whole 4x4x32 slice. The times are simulated.
1024 devices in a mesh: sample: 16 (over z_lo, core), depth: 16 (over y, z_hi), height: 4 (over x).
Axes of the slice: x: 4, y: 4, z: 32 (z_hi: 4, z_lo: 8; z = z_hi * 8 + z_lo), core: 2. Of those that a mesh axis runs over, the one named last changes fastest.
Arguments:
- volume: bfloat16 [256, 16, 16, 16, 128], P('sample', 'depth', 'height'), may hold values from -6 to 6
- conv_weight: bfloat16 [3456, 256], replicated, may hold values from -0.109375 to 0.109375
- dense_weight: bfloat16 [16, 4, 1024, 128], P('depth', 'height'), may hold values from -0.09375 to 0.09375
- mid_weight: float32 [128, 64], replicated, may hold values from -0.5 to 0.5
- out_weight: float32 [64, 4], replicated, may hold values from -0.75 to 0.75
- targets: float32 [256, 4], P('sample'), may hold values from -4 to 4
Outputs:
- predictions: float32 [256, 4], P('sample')
- dense_grad: float32 [16, 4, 1024, 128], P('depth', 'height')
- conv_grad: float32 [3456, 256], P(('depth', 'height'), 'sample')
All inputs are finite; a program needn't handle non-finite values.
Results may differ from a plain program's by a relative error of at most 0.0051.
Values may be sent and summed in bfloat16 or wider, within the bound.
A program may use at most 64 MiB of HBM per device.

v0:
```python
import jax
import jax.numpy as jnp
from jax import lax
from jax.sharding import PartitionSpec as P


def padded_2(cells, sides, width):
    for axis, dim in sides:
        count = lax.axis_size(axis)
        ends = count - 1
        head = lax.slice_in_dim(cells, 0, width, axis=dim)
        tail = lax.slice_in_dim(cells, cells.shape[dim] - width, cells.shape[dim], axis=dim)
        cells = jnp.concatenate(
            [
                lax.ppermute(tail, axis, [(i, (i + 1) % count) for i in range(ends)]),
                cells,
                lax.ppermute(head, axis, [((i + 1) % count, i) for i in range(ends)]),
            ],
            axis=dim,
        )
    return cells


def gelu_slope(value):
    return jax.vjp(lambda v: jax.nn.gelu(v, approximate=True), value)[1](jnp.ones_like(value))[0]


def per_device(volume, conv_weight, dense_weight, mid_weight, out_weight, targets):
    hi = lax.Precision.HIGHEST
    samp, deep, high, wide, chans = volume.shape
    outs = conv_weight.shape[1]
    padded = padded_2(volume, (("depth", 1), ("height", 2)), 1)
    padded = jnp.pad(padded, ((0, 0), (0, 0), (0, 0), (1, 1), (0, 0)))
    pieces = []
    for a in range(3):
        for b in range(3):
            for c in range(3):
                pieces.append(padded[:, a : a + deep, b : b + high, c : c + wide])
    cells = jnp.concatenate(pieces, axis=-1).reshape(samp * deep * high * wide, 27 * chans)
    pre = jnp.dot(cells, conv_weight, preferred_element_type=jnp.float32)
    active = jax.nn.gelu(pre, approximate=True).reshape(
        samp, deep, high // 4, 4, wide // 4, 4, outs
    )
    pooled = jnp.mean(active, axis=(3, 5)).astype(jnp.bfloat16)
    flat = pooled.reshape(samp, -1)
    dense_flat = dense_weight.reshape(-1, dense_weight.shape[-1])
    partial_value = jnp.dot(flat, dense_flat, preferred_element_type=jnp.float32)
    first = lax.psum(partial_value, ("depth", "height"))
    second = jnp.dot(jax.nn.gelu(first, approximate=True), mid_weight, precision=hi)
    predictions = jnp.dot(jax.nn.gelu(second, approximate=True), out_weight, precision=hi)
    slope2 = gelu_slope(second) * jnp.dot(predictions - targets, out_weight.T, precision=hi)
    slope1 = (gelu_slope(first) * jnp.dot(slope2, mid_weight.T, precision=hi)).astype(jnp.bfloat16)
    local_dense = jnp.dot(flat.T, slope1, preferred_element_type=jnp.float32)
    dense_grad = lax.psum(local_dense, "sample").reshape(dense_weight.shape)
    back = jnp.dot(slope1, dense_flat.T, preferred_element_type=jnp.float32)
    spread = back.reshape(samp, deep, high // 4, 1, wide // 4, 1, outs) / 16.0
    spread = jnp.broadcast_to(spread, (samp, deep, high // 4, 4, wide // 4, 4, outs)).reshape(
        -1, outs
    )
    cell_slope = (spread * gelu_slope(pre)).astype(jnp.bfloat16)
    local_kernel = jnp.dot(cells.T, cell_slope, preferred_element_type=jnp.float32)
    by_channel = lax.psum_scatter(local_kernel, "sample", scatter_dimension=1, tiled=True)
    conv_grad = lax.psum_scatter(by_channel, ("depth", "height"), scatter_dimension=0, tiled=True)
    return (predictions, dense_grad, conv_grad)


def solution(mesh):
    in_specs = (
        P("sample", "depth", "height", None, None),
        P(),
        P("depth", "height", None, None),
        P(),
        P(),
        P("sample", None),
    )
    out_specs = (
        P("sample", None),
        P("depth", "height", None, None),
        P(("depth", "height"), "sample"),
    )
    return jax.shard_map(
        per_device, mesh=mesh, in_specs=in_specs, out_specs=out_specs, check_vma=False
    )
```

profile of v0, /device:TPU:1, one launch (start us, length us, event | category | flops | bytes accessed | tf_op | source)
XLA Modules:
  0.0 1814.6 jit_solution(15397559049853520481)
XLA Ops:
  7.2 16.4 collective-permute-start
  23.7 1.3 collective-permute-start.1
  25.0 9.1 collective-permute-done
  34.1 1.0 constant_dynamic-update-slice_fusion.1
  35.1 49.8 %collective-permute-done.1 = bf16[16,1,4,16,128]{4,3,2,1,0:T(8,128)(2,1)S(1)} collective-permute-done((bf16[16,1,4,16,128]{4,3,2,1,0:T(8,128)(2,1)}, bf16[16,1,4,16,128]{4,3,2,1,0:T(8,128)(2,1)S(1)}, u32[]{:S(2)}, u32[]{:S(2)}) %collective-permute-start.1) | collective-permute-done | bytes 262176 | tf_op jit(solution)/shard_map/ppermute | solution.py:17
  85.0 3.1 collective-permute-start.2
  88.1 1.3 collective-permute-start.3
  89.4 1.9 collective-permute-done.2
  91.3 3.8 collective-permute-done.3
  95.2 1.0 fusion.5
  98.8 3.5 multiply_multiply_fusion.2
  102.3 1.5 reshape.50
  103.8 0.4 reduce_sum.9
  104.4 272.4 %psum.14 = f32[16,128]{1,0:T(8,128)S(1)} all-reduce(f32[16,128]{1,0:T(8,128)S(1)} %fusion.25), channel_id=1, replica_groups=mesh['sample'=16,'depth'=16,'height'=4] {'depth','height'}, use_global_device_ids=true, to_apply=%region_1.2 | all-reduce | flops 2048 | bytes 16384 | tf_op jit(solution)/shard_map/psum | solution.py:48
  377.7 0.2 broadcast_in_dim.2
  378.0 1.4 reshape.53
  379.4 7.8 fusion.15
  387.3 123.8 %reduce-scatter.3.cloned.1.call-done = f32[3456,16]{0,1:T(8,128)} async-done(((f32[3456,256]{0,1:T(8,128)}), f32[3456,16]{0,1:T(8,128)}) %reduce-scatter.3.cloned.1.call-update) | async-done | bytes 221200 | tf_op jit(solution)/shard_map/reduce_scatter | solution.py:62
  511.2 1.1 convolution_bitcast_fusion
  512.2 1.3 dynamic-slice
  514.2 1056.3 %all-reduce.7.cloned.1.call-done = f32[3456,16]{0,1:T(8,128)} async-done(((f32[3456,16]{0,1:T(8,128)}), f32[3456,16]{0,1:T(8,128)}) %all-reduce.7.cloned.1.call-update) | async-done | bytes 221200
  1570.4 1.4 constant_dynamic-slice_fusion
  1571.8 234.3 %all-reduce.5.cloned.1.call-done = f32[1,1,1024,128]{3,2,1,0:T(8,128)} async-done(((f32[1,1,1024,128]{3,2,1,0:T(8,128)}), f32[1,1,1024,128]{3,2,1,0:T(8,128)}) %all-reduce.5.cloned.1.call-update) | async-done | bytes 524304 | tf_op jit(solution)/shard_map/psum | solution.py:54
  1806.2 1.9 copy.53
  (61 shorter events, 3.7 us)
Async XLA Ops:
  7.2 91.6 %copy-start = (bf16[3456,256]{1,0:T(8,128)(2,1)S(1)}, bf16[3456,256]{1,0:T(8,128)(2,1)}, u32[]{:S(2)}) copy-start(bf16[3456,256]{1,0:T(8,128)(2,1)} %param.7) | copy-start | bytes 5308420
  7.2 90.2 %copy-start.1 = (bf16[16,1,4,16,128]{4,3,2,1,0:T(8,128)(2,1)S(1)}, bf16[16,1,4,16,128]{4,3,2,1,0:T(8,128)(2,1)}, u32[]{:S(2)}) copy-start(bf16[16,1,4,16,128]{4,3,2,1,0:T(8,128)(2,1)} %param.6) | copy-start | bytes 786436
  7.2 503.9 %reduce-scatter.3.cloned.1.call-start = ((), (), s32[]{:S(2)}) async-start(), calls=%async_computation.2 | async-start | bytes 3760128 | tf_op jit(solution)/shard_map/reduce_scatter | solution.py:62
  7.2 26.8 %collective-permute-start = (bf16[16,1,4,16,128]{4,3,2,1,0:T(8,128)(2,1)}, bf16[16,1,4,16,128]{4,3,2,1,0:T(8,128)(2,1)S(1)}, u32[]{:S(2)}, u32[]{:S(2)}) collective-permute-start(bf16[16,1,4,16,128]{4,3,2,1,0:T(8,128)(2,1)} %param.6), channel_id=1, source_target_pairs={{0,4},{4,8},{8,12},{12,16},{16,20},{20,24},{24,28},{28,32},{32,36}... | collective-permute-start | bytes 786440 | tf_op jit(solution)/shard_map/ppermute | solution.py:15
  23.7 61.3 %collective-permute-start.1 = (bf16[16,1,4,16,128]{4,3,2,1,0:T(8,128)(2,1)}, bf16[16,1,4,16,128]{4,3,2,1,0:T(8,128)(2,1)S(1)}, u32[]{:S(2)}, u32[]{:S(2)}) collective-permute-start(bf16[16,1,4,16,128]{4,3,2,1,0:T(8,128)(2,1)} %param.6), channel_id=1, source_target_pairs={{4,0},{8,4},{12,8},{16,12},{20,16},{24,20},{28,24},{32,28},{36,32}... | collective-permute-start | bytes 786440 | tf_op jit(solution)/shard_map/ppermute | solution.py:17
  85.0 6.3 collective-permute-start.2
  88.1 7.0 collective-permute-start.3
  98.7 3.5 copy-start.4
  98.8 5.5 copy-start.2
  98.8 278.0 %copy-start.3 = (f32[128,64]{0,1:T(8,128)S(1)}, f32[128,64]{0,1:T(8,128)}, u32[]{:S(2)}) copy-start(f32[128,64]{0,1:T(8,128)} %param.9) | copy-start | bytes 98308
  98.8 278.2 %copy-start.5 = (f32[64,4]{0,1:T(4,128)S(1)}, f32[64,4]{0,1:T(4,128)}, u32[]{:S(2)}) copy-start(f32[64,4]{0,1:T(4,128)} %param.10) | copy-start | bytes 3076
  98.8 278.3 %copy-start.6 = (f32[16,4]{0,1:T(4,128)S(1)}, f32[16,4]{0,1:T(4,128)}, u32[]{:S(2)}) copy-start(f32[16,4]{0,1:T(4,128)} %param.11) | copy-start | bytes 772
  377.1 10.1 copy-start.7
  387.2 1183.2 %all-reduce.7.cloned.1.call-start = ((), (), s32[]{:S(2)}) async-start(), calls=%async_computation.3 | async-start | bytes 442368
  511.1 1295.1 %all-reduce.5.cloned.1.call-start = ((), (), s32[]{:S(2)}) async-start(), calls=%async_computation.1 | async-start | bytes 1048576 | tf_op jit(solution)/shard_map/psum | solution.py:54
Sparse Core Ops, SparseCore 0:
  387.4 123.6 reduce-scatter.2
  514.6 1055.8 all-reduce.6
  1574.9 231.2 all-reduce.4
where the time goes:
time: 1810 us
  waiting for transfers between devices  1480 us (82%)
  blocking collectives  272 us (15%)
  starting transfers between devices  22.2 us (1%)
    unnamed x4, waiting for transfers between devices  1060 us
    psum x1, blocking collectives, per_device(): first = lax.psum(partial_value, ('depth', 'height'))  272 us
    psum x1, waiting for transfers between devices, per_device(): dense_grad = lax.psum(local_dense, 'sample').reshape(dense_weight.shape)  234 us
    reduce_scatter x1, waiting for transfers between devices, per_device(): lax.psum_scatter(local_kernel, 'sample', scatter_dimension=1, tiled=True)  124 us
    ppermute x2, waiting for transfers between devices, padded_2(): lax.ppermute(head, axis, [((i + 1) % count, i) for i in range(ends)])  53.7 us
  transfers between devices with their start and end apart: 7, of which 7 were waited for; matrix products, arithmetic and copies ran while one was open for 0% of the time, Pallas kernels for 0%

commit v1 on v0

--- a/solution.py
+++ b/solution.py
@@ -1,7 +1,239 @@
 import jax
 import jax.numpy as jnp
 from jax import lax
+from jax.experimental import pallas as pl
+from jax.experimental.pallas import tpu as pltpu
 from jax.sharding import PartitionSpec as P
+
+F32 = jnp.float32
+BF16 = jnp.bfloat16
+MESH = pl.DeviceIdType.MESH
+
+
+def place():
+    sample, depth, x = lax.axis_index("sample"), lax.axis_index("depth"), lax.axis_index("height")
+    return sample // 2, sample % 2, depth // 4, depth % 4, x
+
+
+def partner(kind, step):
+    z_lo, core, y, z_hi, x = place()
+    if kind == "z_lo":
+        z_lo = (z_lo + step) % 8
+    elif kind == "core":
+        core = (core + step) % 2
+    elif kind == "y":
+        y = (y + step) % 4
+    elif kind == "z_hi":
+        z_hi = (z_hi + step) % 4
+    else:
+        x = (x + step) % 4
+    return (z_lo * 2 + core, y * 4 + z_hi, x)
+
+
+def greet(partners):
+    barrier = pltpu.get_barrier_semaphore()
+    for kind, step in partners:
+        pl.semaphore_signal(barrier, inc=1, device_id=partner(kind, step), device_id_type=MESH)
+
+
+def met(partners):
+    pl.semaphore_wait(pltpu.get_barrier_semaphore(), len(partners))
+
+
+QUADS = [(kind, step) for kind in ("x", "y", "z_hi") for step in (1, 2, 3)]
+OCTETS = [("z_lo", step) for step in range(1, 8)]
+
+
+def first_kernel(part_ref, first_ref, held, send_sem, recv_sem):
+    z_lo, core, y, z_hi, x = place()
+    greet(QUADS)
+    met(QUADS)
+    total = part_ref[...]
+    for stage, (kind, mine) in enumerate((("x", x), ("y", y), ("z_hi", z_hi))):
+        held[stage, mine] = total
+        copies = []
+        for step in (1, 2, 3):
+            at = stage * 3 + step - 1
+            copy = pltpu.make_async_remote_copy(
+                src_ref=held.at[stage, mine],
+                dst_ref=held.at[stage, mine],
+                send_sem=send_sem.at[at],
+                recv_sem=recv_sem.at[at],
+                device_id=partner(kind, step),
+                device_id_type=MESH,
+            )
+            copy.start()
+            copies.append(copy)
+        for copy in copies:
+            copy.wait()
+        total = (held[stage, 0] + held[stage, 1]) + (held[stage, 2] + held[stage, 3])
+    first_ref[...] = total
+
+
+def sum_first(part):
+    return pl.pallas_call(
+        first_kernel,
+        name="sum_first",
+        out_shape=jax.ShapeDtypeStruct(part.shape, F32),
+        in_specs=[pl.BlockSpec(memory_space=pltpu.VMEM)],
+        out_specs=pl.BlockSpec(memory_space=pltpu.VMEM),
+        scratch_shapes=[
+            pltpu.VMEM((3, 4) + part.shape, F32),
+            pltpu.SemaphoreType.DMA((9,)),
+            pltpu.SemaphoreType.DMA((9,)),
+        ],
+        compiler_params=pltpu.CompilerParams(collective_id=0, has_side_effects=True),
+    )(part)
+
+
+GRAD_PARTNERS = [("core", 1)] + QUADS + OCTETS
+
+
+def grads_kernel(
+    kern_ref, pooled_ref, slope_ref, dense_ref, conv_ref,
+    core_in, y_out, y_in, y_sum, x_out, x_in, lo_out, lo_in, hi_out, hi_in,
+    feat, feat_pair, slopes, slopes_pair, piece, pieces, pieces_pair,
+    send_sem, recv_sem,
+):
+    z_lo, core, y, z_hi, x = place()
+    used = [0]
+
+    def copy_to(kind, step, src, dst):
+        at = used[0]
+        used[0] += 1
+        copy = pltpu.make_async_remote_copy(
+            src_ref=src, dst_ref=dst, send_sem=send_sem.at[at], recv_sem=recv_sem.at[at],
+            device_id=partner(kind, step), device_id_type=MESH,
+        )
+        copy.start()
+        return copy
+
+    greet(GRAD_PARTNERS)
+    met(GRAD_PARTNERS)
+    mine = pl.ds(pl.multiple_of(core * 128, 128), 128)
+    theirs = pl.ds(pl.multiple_of(128 - core * 128, 128), 128)
+    core_copies = []
+    for step in (1, 2, 3, 0):
+        to = (y + step) % 4
+        core_copies.append(
+            copy_to("core", 1, kern_ref.at[to, :, theirs], core_in.at[to])
+        )
+    feat[z_lo] = pooled_ref[:, pl.ds(pl.multiple_of(z_lo * 128, 128), 128)]
+    slopes[z_lo] = slope_ref[...]
+    lo_copies = []
+    for kind, step in OCTETS:
+        to = (z_lo + step) % 8
+        lo_copies.append(
+            copy_to(kind, step, pooled_ref.at[:, pl.ds(pl.multiple_of(to * 128, 128), 128)], feat.at[z_lo])
+        )
+        lo_copies.append(copy_to(kind, step, slope_ref, slopes.at[z_lo]))
+    y_copies = []
+    for turn, step in enumerate((1, 2, 3, 0)):
+        to = (y + step) % 4
+        core_copies[turn].wait_recv()
+        total = kern_ref[to, :, mine].astype(F32) + core_in[to].astype(F32)
+        if step:
+            y_out[step - 1] = total.astype(BF16)
+            y_copies.append(copy_to("y", step, y_out.at[step - 1], y_in.at[step - 1]))
+        else:
+            y_sum[0:864] = total
+    y_sum[864:896] = jnp.zeros((32, 128), F32)
+    for copy in lo_copies:
+        copy.wait()
+    pair = [copy_to("core", 1, feat, feat_pair), copy_to("core", 1, slopes, slopes_pair)]
+    for copy in pair:
+        copy.wait()
+    over = (((0,), (0,)), ((), ()))
+    grad = lax.dot_general(
+        feat[...].reshape(128, 128), slopes[...].reshape(128, 128), over, preferred_element_type=F32
+    ) + lax.dot_general(
+        feat_pair[...].reshape(128, 128), slopes_pair[...].reshape(128, 128), over, preferred_element_type=F32
+    )
+    piece[...] = grad
+    own = piece[pl.ds(pl.multiple_of(core * 64, 64), 64)].astype(BF16)
+    pieces[z_lo] = own
+    piece_copies = [copy_to(kind, step, pieces.at[z_lo], pieces.at[z_lo]) for kind, step in OCTETS]
+    for copy in y_copies:
+        copy.wait()
+    y_sum[0:864] = (y_sum[0:864] + y_in[0].astype(F32)) + (y_in[1].astype(F32) + y_in[2].astype(F32))
+    for hi in range(4):
+        for to in range(4):
+            start = (hi * 4 + to) * 54
+            x_out[to, hi] = y_sum[start : start + 64].astype(BF16)
+    x_copies = []
+    for step in (1, 2, 3):
+        x_copies.append(copy_to("x", step, x_out.at[(x + step) % 4], x_in.at[step - 1]))
+    for copy in x_copies:
+        copy.wait()
+    blocks = (x_out[x].astype(F32) + x_in[0].astype(F32)) + (x_in[1].astype(F32) + x_in[2].astype(F32))
+    for half in range(2):
+        both = jnp.concatenate([blocks[2 * half].T, blocks[2 * half + 1].T], axis=1)
+        lo_out[:, half] = both.reshape(8, 16, 128).astype(BF16)
+    turn_copies = []
+    for kind, step in OCTETS:
+        turn_copies.append(copy_to(kind, step, lo_out.at[(z_lo + step) % 8], lo_in.at[step - 1]))
+    for copy in turn_copies:
+        copy.wait()
+    total = lo_out[z_lo].astype(F32)
+    for step in range(7):
+        total = total + lo_in[step].astype(F32)
+    hi_out[...] = total
+    hi_copies = []
+    for step in (1, 2, 3):
+        hi_copies.append(copy_to("z_hi", step, hi_out.at[((z_hi + step) % 4) // 2], hi_in.at[step - 1]))
+    for copy in piece_copies:
+        copy.wait()
+    last = copy_to("core", 1, pieces, pieces_pair)
+    last.wait()
+    for at in range(8):
+        dense_ref[pl.ds(pl.multiple_of(at * 128 + core * 64, 64), 64)] = pieces[at].astype(F32)
+        dense_ref[pl.ds(pl.multiple_of(at * 128 + 64 - core * 64, 64), 64)] = pieces_pair[at].astype(F32)
+    for copy in hi_copies:
+        copy.wait()
+    total = (hi_out[z_hi // 2] + hi_in[0]) + (hi_in[1] + hi_in[2])
+    turned = total.T
+    conv_ref[...] = jnp.where(z_hi % 2 == 0, turned[0:54], turned[64:118])
+    for copy in core_copies:
+        copy.wait_send()
+
+
+def sum_grads(kern, pooled, slope1):
+    any_vmem = pl.BlockSpec(memory_space=pltpu.VMEM)
+    copies = 4 + 14 + 3 + 2 + 7 + 3 + 7 + 3 + 1
+    return pl.pallas_call(
+        grads_kernel,
+        name="sum_grads",
+        out_shape=(
+            jax.ShapeDtypeStruct((1024, 128), F32),
+            jax.ShapeDtypeStruct((54, 16), F32),
+        ),
+        in_specs=[any_vmem] * 3,
+        out_specs=(any_vmem, any_vmem),
+        scratch_shapes=[
+            pltpu.VMEM((4, 864, 128), BF16),
+            pltpu.VMEM((3, 864, 128), BF16),
+            pltpu.VMEM((3, 864, 128), BF16),
+            pltpu.VMEM((896, 128), F32),
+            pltpu.VMEM((4, 4, 64, 128), BF16),
+            pltpu.VMEM((3, 4, 64, 128), BF16),
+            pltpu.VMEM((8, 2, 16, 128), BF16),
+            pltpu.VMEM((7, 2, 16, 128), BF16),
+            pltpu.VMEM((2, 16, 128), F32),
+            pltpu.VMEM((3, 16, 128), F32),
+            pltpu.VMEM((8, 16, 128), BF16),
+            pltpu.VMEM((8, 16, 128), BF16),
+            pltpu.VMEM((8, 16, 128), BF16),
+            pltpu.VMEM((8, 16, 128), BF16),
+            pltpu.VMEM((128, 128), F32),
+            pltpu.VMEM((8, 64, 128), BF16),
+            pltpu.VMEM((8, 64, 128), BF16),
+            pltpu.SemaphoreType.DMA((copies,)),
+            pltpu.SemaphoreType.DMA((copies,)),
+        ],
+        compiler_params=pltpu.CompilerParams(
+            collective_id=1, has_side_effects=True, vmem_limit_bytes=40 * 2**20
+        ),
+    )(kern, pooled, slope1)
 
 
 def padded_2(cells, sides, width):
@@ -45,23 +277,22 @@
     flat = pooled.reshape(samp, -1)
     dense_flat = dense_weight.reshape(-1, dense_weight.shape[-1])
     partial_value = jnp.dot(flat, dense_flat, preferred_element_type=jnp.float32)
-    first = lax.psum(partial_value, ("depth", "height"))
+    first = sum_first(partial_value)
     second = jnp.dot(jax.nn.gelu(first, approximate=True), mid_weight, precision=hi)
     predictions = jnp.dot(jax.nn.gelu(second, approximate=True), out_weight, precision=hi)
     slope2 = gelu_slope(second) * jnp.dot(predictions - targets, out_weight.T, precision=hi)
     slope1 = (gelu_slope(first) * jnp.dot(slope2, mid_weight.T, precision=hi)).astype(jnp.bfloat16)
-    local_dense = jnp.dot(flat.T, slope1, preferred_element_type=jnp.float32)
-    dense_grad = lax.psum(local_dense, "sample").reshape(dense_weight.shape)
     back = jnp.dot(slope1, dense_flat.T, preferred_element_type=jnp.float32)
     spread = back.reshape(samp, deep, high // 4, 1, wide // 4, 1, outs) / 16.0
     spread = jnp.broadcast_to(spread, (samp, deep, high // 4, 4, wide // 4, 4, outs)).reshape(
         -1, outs
     )
     cell_slope = (spread * gelu_slope(pre)).astype(jnp.bfloat16)
+    cell_slope = cell_slope.reshape(-1, 8, 2, 16).swapaxes(1, 2).reshape(-1, outs)
     local_kernel = jnp.dot(cells.T, cell_slope, preferred_element_type=jnp.float32)
-    by_channel = lax.psum_scatter(local_kernel, "sample", scatter_dimension=1, tiled=True)
-    conv_grad = lax.psum_scatter(by_channel, ("depth", "height"), scatter_dimension=0, tiled=True)
-    return (predictions, dense_grad, conv_grad)
+    kern = local_kernel.astype(BF16).reshape(4, 864, outs)
+    dense_grad, conv_grad = sum_grads(kern, flat, slope1)
+    return (predictions, dense_grad.reshape(dense_weight.shape), conv_grad)
 
 
 def solution(mesh):

time: 1810 us -> 192 us (0.11)
  waiting for transfers between devices: 1480 us -> 64.7 us
  blocking collectives: 272 us -> 0 us
  Pallas kernels: 0 us -> 79.5 us
    unnamed x4 -> x0, waiting for transfers between devices: 1060 us -> none
    psum x1 -> x0, blocking collectives: 272 us -> none  [per_device(): first = lax.psum(partial_value, ('depth', 'height'))]
    psum x1 -> x0, waiting for transfers between devices: 234 us -> none  [per_device(): dense_grad = lax.psum(local_dense, 'sample').reshape(dense_weight.shape)]
    reduce_scatter x1 -> x0, waiting for transfers between devices: 124 us -> none  [per_device(): lax.psum_scatter(local_kernel, 'sample', scatter_dimension=1, tiled=True)]
    pallas_call x0 -> x2, Pallas kernels: none -> 79.5 us  [the longest x1 48.4 us: sum_grads(): pl.pallas_call(grads_kernel, name='sum_grads', out_shape=(jax.ShapeDtypeS...]
  transfers between devices with their start and end apart: 7 -> 4, of which waited for: 7 -> 4; matrix products, arithmetic and copies ran while one was open for 0% -> 1% of each run, Pallas kernels for 0% -> 0%
where the time goes in v1:
time: 192 us
  Pallas kernels  79.5 us (41%)
  waiting for transfers between devices  64.7 us (34%)
  starting transfers between devices  22.1 us (12%)
  matrix products  11.6 us (6%)
  local copies, waits for them, and re-layouts  9.25 us (5%)
  other arithmetic  3.71 us (2%)
    ppermute x2, waiting for transfers between devices, padded_2(): lax.ppermute(head, axis, [((i + 1) % count, i) for i in range(ends)])  53.7 us
    pallas_call x1, Pallas kernels, sum_grads(): pl.pallas_call(grads_kernel, name='sum_grads', out_shape=(jax.ShapeDtypeS...  48.4 us
    pallas_call x1, Pallas kernels, sum_first(): pl.pallas_call(first_kernel, name='sum_first', out_shape=jax.ShapeDtypeSt...  31.1 us
    ppermute x2, starting transfers between devices, padded_2(): lax.ppermute(tail, axis, [(i, (i + 1) % count) for i in range(ends)])  19.5 us
    ppermute x2, waiting for transfers between devices, padded_2(): lax.ppermute(tail, axis, [(i, (i + 1) % count) for i in range(ends)])  11 us
    dot_general x1, matrix products, per_device(): jnp.dot(cells.T, cell_slope, preferred_element_type=jnp.float32)  5.08 us
    unnamed x40, local copies, waits for them, and re-layouts  4.33 us
  transfers between devices with their start and end apart: 4, of which 4 were waited for; matrix products, arithmetic and copies ran while one was open for 1% of the time, Pallas kernels for 0%

profile of v1, /device:TPU:1, one launch (start us, length us, event | category | flops | bytes accessed | tf_op | source)
XLA Modules:
  0.0 191.9 jit_solution(7558163371155089820)
XLA Ops:
  0.7 16.4 %collective-permute-start = (bf16[16,1,4,16,128]{4,3,2,1,0:T(8,128)(2,1)}, bf16[16,1,4,16,128]{4,3,2,1,0:T(8,128)(2,1)S(1)}, u32[]{:S(2)}, u32[]{:S(2)}) collective-permute-start(bf16[16,1,4,16,128]{4,3,2,1,0:T(8,128)(2,1)} %param.6), channel_id=1, source_target_pairs={{0,4},{4,8},{8,12},{12,16},{16,20},{20,24},{24,28},{28,32},{32,36}... | collective-permute-start | bytes 786440 | tf_op jit(solution)/shard_map/ppermute | solution.py:247
  17.1 1.3 collective-permute-start.1
  18.4 9.1 %collective-permute-done = bf16[16,1,4,16,128]{4,3,2,1,0:T(8,128)(2,1)S(1)} collective-permute-done((bf16[16,1,4,16,128]{4,3,2,1,0:T(8,128)(2,1)}, bf16[16,1,4,16,128]{4,3,2,1,0:T(8,128)(2,1)S(1)}, u32[]{:S(2)}, u32[]{:S(2)}) %collective-permute-start) | collective-permute-done | bytes 262176 | tf_op jit(solution)/shard_map/ppermute | solution.py:247
  27.5 1.0 constant_dynamic-update-slice_fusion.1
  28.5 49.8 %collective-permute-done.1 = bf16[16,1,4,16,128]{4,3,2,1,0:T(8,128)(2,1)S(1)} collective-permute-done((bf16[16,1,4,16,128]{4,3,2,1,0:T(8,128)(2,1)}, bf16[16,1,4,16,128]{4,3,2,1,0:T(8,128)(2,1)S(1)}, u32[]{:S(2)}, u32[]{:S(2)}) %collective-permute-start.1) | collective-permute-done | bytes 262176 | tf_op jit(solution)/shard_map/ppermute | solution.py:249
  78.4 3.1 %collective-permute-start.2 = (bf16[16,3,1,16,128]{4,3,2,1,0:T(8,128)(2,1)S(1)}, bf16[16,3,1,16,128]{4,3,2,1,0:T(8,128)(2,1)S(1)}, u32[]{:S(2)}, u32[]{:S(2)}) collective-permute-start(bf16[16,3,1,16,128]{4,3,2,1,0:T(8,128)(2,1)S(1)} %get-tuple-element.16), channel_id=1, source_target_pairs={{0,1},{1,2},{2,3},{4,5},{5,6},{6,7},{8,9},{9,10},{10,11},{12,13},{... | collective-permute-start | bytes 589832 | tf_op jit(solution)/shard_map/ppermute | solution.py:247
  81.5 1.3 collective-permute-start.3
  82.8 1.9 collective-permute-done.2
  84.8 3.8 %collective-permute-done.3 = bf16[16,3,1,16,128]{4,3,2,1,0:T(8,128)(2,1)S(1)} collective-permute-done((bf16[16,3,1,16,128]{4,3,2,1,0:T(8,128)(2,1)S(1)}, bf16[16,3,1,16,128]{4,3,2,1,0:T(8,128)(2,1)S(1)}, u32[]{:S(2)}, u32[]{:S(2)}) %collective-permute-start.3) | collective-permute-done | bytes 196640 | tf_op jit(solution)/shard_map/ppermute | solution.py:249
  88.6 1.0 fusion.5
  92.2 3.5 %multiply_multiply_fusion.2 = (f32[1024,256]{1,0:T(8,128)}, f32[1024,256]{1,0:T(8,128)}) fusion(bf16[1024,3456]{1,0:T(8,128)(2,1)S(1)} %bitcast.37, bf16[3456,256]{1,0:T(8,128)(2,1)S(1)} %copy-done), kind=kOutput, calls=%fused_computation.23 | convolution fusion | flops 1814036480 | bytes 10944512 | tf_op jit(solution)/shard_map/dot_general | solution.py:272
  95.7 1.5 reshape.59
  97.3 0.4 reduce_sum.9
  97.7 0.8 fusion.17.part_ref
  98.4 31.1 %sum_first.1 = f32[16,128]{1,0:T(8,128)} custom-call(f32[16,128]{1,0:T(8,128)} %fusion.17.part_ref), custom_call_target="tpu_custom_call" | custom-call | tf_op jit(solution)/shard_map/sum_first/pallas_call | solution.py:74
  129.6 0.8 fusion.35
  130.8 0.8 fusion.6.slope_ref
  131.9 1.3 broadcast_in_dim.2
  133.2 1.6 reshape.61
  134.8 1.9 fusion.14
  136.9 5.1 %convolution_convert_fusion = bf16[3456,256]{1,0:T(8,128)(2,1)S(1)} fusion(bf16[1024,3456]{1,0:T(8,128)(2,1)} %bitcast.38, bf16[1024,256]{0,1:T(8,128)(2,1)S(1)} %bitcast.36), kind=kOutput, calls=%fused_computation.2 | convolution fusion | flops 1812824064 | bytes 9371648 | tf_op jit(solution)/shard_map/dot_general | solution.py:292
  142.0 48.4 %sum_grads.1 = (f32[1024,128]{1,0:T(8,128)S(1)}, f32[54,16]{1,0:T(8,128)S(1)}) custom-call(bf16[4,864,256]{2,1,0:T(8,128)(2,1)S(1)} %bitcast.30, bf16[16,1024]{1,0:T(8,128)(2,1)S(1)} %bitcast.33, bf16[16,128]{1,0:T(8,128)(2,1)S(1)} %fusion.6.slope_ref), custom_call_target="tpu_custom_call" | custom-call | tf_op jit(solution)/shard_map/sum_grads/pallas_call | solution.py:203
  190.4 0.7 copy.22
  191.1 0.8 copy.58
  (54 shorter events, 3.3 us)
Async XLA Ops:
  0.6 91.5 %copy-start = (bf16[3456,256]{1,0:T(8,128)(2,1)S(1)}, bf16[3456,256]{1,0:T(8,128)(2,1)}, u32[]{:S(2)}) copy-start(bf16[3456,256]{1,0:T(8,128)(2,1)} %param.7) | copy-start | bytes 5308420
  0.6 90.2 %copy-start.1 = (bf16[16,1,4,16,128]{4,3,2,1,0:T(8,128)(2,1)S(1)}, bf16[16,1,4,16,128]{4,3,2,1,0:T(8,128)(2,1)}, u32[]{:S(2)}) copy-start(bf16[16,1,4,16,128]{4,3,2,1,0:T(8,128)(2,1)} %param.6) | copy-start | bytes 786436
  0.7 26.8 %collective-permute-start = (bf16[16,1,4,16,128]{4,3,2,1,0:T(8,128)(2,1)}, bf16[16,1,4,16,128]{4,3,2,1,0:T(8,128)(2,1)S(1)}, u32[]{:S(2)}, u32[]{:S(2)}) collective-permute-start(bf16[16,1,4,16,128]{4,3,2,1,0:T(8,128)(2,1)} %param.6), channel_id=1, source_target_pairs={{0,4},{4,8},{8,12},{12,16},{16,20},{20,24},{24,28},{28,32},{32,36}... | collective-permute-start | bytes 786440 | tf_op jit(solution)/shard_map/ppermute | solution.py:247
  17.1 61.3 %collective-permute-start.1 = (bf16[16,1,4,16,128]{4,3,2,1,0:T(8,128)(2,1)}, bf16[16,1,4,16,128]{4,3,2,1,0:T(8,128)(2,1)S(1)}, u32[]{:S(2)}, u32[]{:S(2)}) collective-permute-start(bf16[16,1,4,16,128]{4,3,2,1,0:T(8,128)(2,1)} %param.6), channel_id=1, source_target_pairs={{4,0},{8,4},{12,8},{16,12},{20,16},{24,20},{28,24},{32,28},{36,32}... | collective-permute-start | bytes 786440 | tf_op jit(solution)/shard_map/ppermute | solution.py:249
  78.4 6.3 %collective-permute-start.2 = (bf16[16,3,1,16,128]{4,3,2,1,0:T(8,128)(2,1)S(1)}, bf16[16,3,1,16,128]{4,3,2,1,0:T(8,128)(2,1)S(1)}, u32[]{:S(2)}, u32[]{:S(2)}) collective-permute-start(bf16[16,3,1,16,128]{4,3,2,1,0:T(8,128)(2,1)S(1)} %get-tuple-element.16), channel_id=1, source_target_pairs={{0,1},{1,2},{2,3},{4,5},{5,6},{6,7},{8,9},{9,10},{10,11},{12,13},{... | collective-permute-start | bytes 589832 | tf_op jit(solution)/shard_map/ppermute | solution.py:247
  81.5 7.0 %collective-permute-start.3 = (bf16[16,3,1,16,128]{4,3,2,1,0:T(8,128)(2,1)S(1)}, bf16[16,3,1,16,128]{4,3,2,1,0:T(8,128)(2,1)S(1)}, u32[]{:S(2)}, u32[]{:S(2)}) collective-permute-start(bf16[16,3,1,16,128]{4,3,2,1,0:T(8,128)(2,1)S(1)} %get-tuple-element.17), channel_id=1, source_target_pairs={{1,0},{2,1},{3,2},{5,4},{6,5},{7,6},{9,8},{10,9},{11,10},{13,12},{... | collective-permute-start | bytes 589832 | tf_op jit(solution)/shard_map/ppermute | solution.py:249
  92.2 3.6 %copy-start.4 = (bf16[16,1,4,16,3456]{4,3,2,1,0:T(8,128)(2,1)}, bf16[16,1,4,16,3456]{4,3,2,1,0:T(8,128)(2,1)S(1)}, u32[]{:S(2)}) copy-start(bf16[16,1,4,16,3456]{4,3,2,1,0:T(8,128)(2,1)S(1)} %slice_dynamic-update-slice_fusion) | copy-start | bytes 21233668
  92.2 5.5 %copy-start.2 = (bf16[1,1,1024,128]{3,2,1,0:T(8,128)(2,1)S(1)}, bf16[1,1,1024,128]{3,2,1,0:T(8,128)(2,1)}, u32[]{:S(2)}) copy-start(bf16[1,1,1024,128]{3,2,1,0:T(8,128)(2,1)} %param.8) | copy-start | bytes 786436
  92.2 37.4 %copy-start.3 = (f32[128,64]{0,1:T(8,128)S(1)}, f32[128,64]{0,1:T(8,128)}, u32[]{:S(2)}) copy-start(f32[128,64]{0,1:T(8,128)} %param.9) | copy-start | bytes 98308
  92.2 38.2 %copy-start.5 = (f32[64,4]{0,1:T(4,128)S(1)}, f32[64,4]{0,1:T(4,128)}, u32[]{:S(2)}) copy-start(f32[64,4]{0,1:T(4,128)} %param.10) | copy-start | bytes 3076
  92.2 38.4 %copy-start.6 = (f32[16,4]{0,1:T(4,128)S(1)}, f32[16,4]{0,1:T(4,128)}, u32[]{:S(2)}) copy-start(f32[16,4]{0,1:T(4,128)} %param.11) | copy-start | bytes 772
  130.6 11.4 %copy-start.7 = (f32[16,4]{0,1:T(4,128)}, f32[16,4]{0,1:T(4,128)S(1)}, u32[]{:S(2)}) copy-start(f32[16,4]{0,1:T(4,128)S(1)} %fusion.33) | copy-start | bytes 772

commit v2 on v0

v2 whole, which is shorter than its diff:
```python
import jax
import jax.numpy as jnp
from jax import lax
from jax.experimental import pallas as pl
from jax.experimental.pallas import tpu as pltpu
from jax.sharding import PartitionSpec as P

F32 = jnp.float32
BF16 = jnp.bfloat16
MESH = pl.DeviceIdType.MESH
EXACT = lax.Precision.HIGHEST


def place():
    sample, depth, x = lax.axis_index("sample"), lax.axis_index("depth"), lax.axis_index("height")
    return sample // 2, sample % 2, depth // 4, depth % 4, x


def partner(kind, step):
    z_lo, core, y, z_hi, x = place()
    if kind == "z_lo":
        z_lo = (z_lo + step) % 8
    elif kind == "z_four":
        z_lo = (z_lo // 4) * 4 + (z_lo + step) % 4
    elif kind == "core":
        core = (core + step) % 2
    elif kind == "y":
        y = (y + step) % 4
    elif kind == "z_hi":
        z_hi = (z_hi + step) % 4
    else:
        x = (x + step) % 4
    return (z_lo * 2 + core, y * 4 + z_hi, x)


QUADS = [(kind, step) for kind in ("x", "y", "z_hi") for step in (1, 2, 3)]
OCTETS = [("z_lo", step) for step in range(1, 8)]
PARTNERS = [("core", 1)] + QUADS + OCTETS
COPIES = 128


def gelu_and_slope(value):
    rate = 0.7978845608028654
    square = value * value
    bend = jnp.tanh(rate * (value + 0.044715 * value * square))
    half = 0.5 * (1.0 + bend)
    slope = half + 0.5 * value * (1.0 - bend * bend) * (rate * (1.0 + 3 * 0.044715 * square))
    return value * half, slope


def one_hot(shape, test, kind, weight=1.0):
    row = lax.broadcasted_iota(jnp.int32, shape, 0)
    column = lax.broadcasted_iota(jnp.int32, shape, 1)
    return jnp.where(test(row, column), weight, 0.0).astype(kind)


def kernel(
    vol_ref, weight_ref, dense_w_ref, mid_ref, out_w_ref, targets_ref,
    pred_ref, dense_ref, conv_ref,
    ext, wide, slope_at, summed, pool, pool_out, gathered, held, back, turned, preds,
    kern, core_in, y_out, y_in, y_sum, x_out, x_in, lo_out, lo_in, hi_out, hi_in,
    feat, feat_pair, slopes, slopes_pair, part_out, part_in, pieces, pieces_pair,
    send_sem, recv_sem, local_sem,
):
    z_lo, core, y, z_hi, x = place()
    used = [0]

    def reserve(count):
        used[0] += count
        assert used[0] <= COPIES
        return used[0] - count

    def copy_to(kind, step, src, dst):
        at = reserve(1)
        copy = pltpu.make_async_remote_copy(
            src_ref=src, dst_ref=dst, send_sem=send_sem.at[at], recv_sem=recv_sem.at[at],
            device_id=partner(kind, step), device_id_type=MESH,
        )
        copy.start()
        return copy

    barrier = pltpu.get_barrier_semaphore()
    for kind, step in PARTNERS:
        pl.semaphore_signal(barrier, inc=1, device_id=partner(kind, step), device_id_type=MESH)
    own = pltpu.make_async_copy(vol_ref.at[pl.ds(z_hi * 4, 4)], ext.at[:, 1 + z_hi, 1:5], local_sem)
    own.start()
    own.wait()
    pl.semaphore_wait(barrier, len(PARTNERS))

    vol_copies = []
    for step in (2, 1, 3):
        to = (z_hi + step) % 4
        vol_copies.append(
            copy_to("z_hi", step, vol_ref.at[pl.ds(to * 4, 4)], ext.at[:, 1 + z_hi, 1:5])
        )
    share = pl.ds(pl.multiple_of(core * 512 + (z_lo % 4) * 128, 128), 128)
    hi_weights = [
        copy_to("z_hi", step, dense_w_ref.at[share], gathered.at[step - 1, share]) for step in (2, 1, 3)
    ]
    for copy in vol_copies:
        copy.wait_recv()
    y_halo = [
        copy_to("y", 1, ext.at[:, 4, 1:5], ext.at[:, 0, 1:5]),
        copy_to("y", 3, ext.at[:, 1, 1:5], ext.at[:, 5, 1:5]),
    ]
    x_halo = [
        copy_to("x", 1, ext.at[:, 1:5, 4], ext.at[:, 1:5, 0]),
        copy_to("x", 3, ext.at[:, 1:5, 1], ext.at[:, 1:5, 5]),
    ]
    for copy, at in zip(y_halo, (0, 5)):
        copy.wait_recv()
        x_halo.append(copy_to("x", 1, ext.at[:, at, 4], ext.at[:, at, 0]))
        x_halo.append(copy_to("x", 3, ext.at[:, at, 1], ext.at[:, at, 5]))
    for copy in hi_weights:
        copy.wait_recv()
    lo_weights = [
        copy_to("z_four", step, gathered.at[:, share], gathered.at[:, share]) for step in (1, 2, 3)
    ]
    for copy in x_halo:
        copy.wait()
    for copy in vol_copies + y_halo + hi_weights:
        copy.wait_send()

    @pl.when(y == 0)
    def _():
        ext[:, 0] = jnp.zeros((4, 6, 16, 128), BF16)

    @pl.when(y == 3)
    def _():
        ext[:, 5] = jnp.zeros((4, 6, 16, 128), BF16)

    @pl.when(x == 0)
    def _():
        ext[:, :, 0] = jnp.zeros((4, 6, 16, 128), BF16)

    @pl.when(x == 3)
    def _():
        ext[:, :, 5] = jnp.zeros((4, 6, 16, 128), BF16)

    def forward(s, carry):
        cells = ext[s].reshape(36, 16, 128).astype(F32)
        edge = jnp.zeros((36, 1, 128), F32)
        wide[s, :, :, :, 0:128] = (
            jnp.concatenate([edge, cells[:, :15]], axis=1).astype(BF16).reshape(6, 6, 16, 128)
        )
        wide[s, :, :, :, 128:256] = ext[s]
        wide[s, :, :, :, 256:384] = (
            jnp.concatenate([cells[:, 1:], edge], axis=1).astype(BF16).reshape(6, 6, 16, 128)
        )
        pre = jnp.zeros((256, 256), F32)
        for tap in range(9):
            a, b = tap // 3, tap % 3
            pre = pre + jnp.dot(
                wide[s, a : a + 4, b : b + 4].reshape(256, 384),
                weight_ref[tap * 384 : tap * 384 + 384],
                preferred_element_type=F32,
            )
        active, slope = gelu_and_slope(pre)
        slope_at[s] = slope
        summed[s] = jnp.sum(active.reshape(4, 4, 16, 256), axis=1).reshape(64, 256)
        return carry

    lax.fori_loop(0, 4, forward, 0)
    for copy in lo_weights:
        copy.wait()
    half_rows = pl.ds(pl.multiple_of(core * 512, 512), 512)
    pair_weights = copy_to("core", 1, gathered.at[:, half_rows], gathered.at[:, half_rows])

    spread = one_hot(
        (256, 256),
        lambda r, c: (r // 64 == c // 16 % 4)
        & (r // 16 % 4 == c % 16 // 4)
        & (r % 16 == z_hi * 4 + c // 64),
        F32,
        1.0 / 16,
    )
    pooled = jnp.dot(
        spread, summed[...].reshape(256, 256), precision=EXACT, preferred_element_type=F32
    ).astype(BF16)
    pool[...] = pooled.reshape(4, 4, 16, 256)
    order = one_hot(
        (64, 256),
        lambda r, c: (r // 16 == c // 16 % 4)
        & (r // 4 % 4 == c // 64)
        & (z_hi * 4 + r % 4 == c % 16),
        BF16,
    )
    pool_out[...] = (
        jnp.dot(order, pooled, preferred_element_type=F32).astype(BF16).reshape(4, 16, 256)
    )

    def features(at):
        return pool_out.at[at // 2, :, pl.ds(pl.multiple_of(at % 2 * 128, 128), 128)]

    feat_own = pltpu.make_async_copy(features(z_lo), feat.at[z_lo], local_sem)
    feat_own.start()
    feat_copies = [
        copy_to(kind, step, features((z_lo + step) % 8), feat.at[z_lo]) for kind, step in OCTETS
    ]
    feat_own.wait()
    total = jnp.zeros((16, 128), F32)
    for k in range(4):
        if k == 1:
            pair_weights.wait()
        for block in range(4):
            rows = slice(block * 256, block * 256 + 256)
            total = total + jnp.dot(
                pool[(z_hi - k + 4) % 4, block],
                dense_w_ref[rows] if k == 0 else gathered[k - 1, rows],
                preferred_element_type=F32,
            )
    for stage, (kind, mine) in enumerate((("x", x), ("y", y))):
        held[stage, mine] = total
        copies = [
            copy_to(kind, step, held.at[stage, mine], held.at[stage, mine]) for step in (1, 2, 3)
        ]
        for copy in copies:
            copy.wait()
        total = (held[stage, 0] + held[stage, 1]) + (held[stage, 2] + held[stage, 3])
    first = total
    out_w = jnp.concatenate([out_w_ref[...], jnp.zeros((64, 124), F32)], axis=1)
    targets = jnp.concatenate([targets_ref[...], jnp.zeros((16, 124), F32)], axis=1)
    across = (((1,), (1,)), ((), ()))
    first_gelu, first_slope = gelu_and_slope(first)
    second = jnp.dot(first_gelu, mid_ref[...], precision=EXACT, preferred_element_type=F32)
    second_gelu, second_slope = gelu_and_slope(second)
    pred = jnp.dot(second_gelu, out_w, precision=EXACT, preferred_element_type=F32)
    slope2 = second_slope * lax.dot_general(
        pred - targets, out_w, across, precision=EXACT, preferred_element_type=F32
    )
    slope1 = first_slope * lax.dot_general(
        slope2, mid_ref[...], across, precision=EXACT, preferred_element_type=F32
    )
    ours = lax.broadcasted_iota(jnp.int32, (16, 128), 0) // 4 == z_hi
    slope1 = jnp.where(ours, slope1, 0.0).astype(BF16)
    preds[z_hi] = jnp.where(ours, pred, 0.0)
    repeat = one_hot((16, 16), lambda r, c: z_hi * 4 + r % 4 == c, BF16)
    slopes[z_lo] = jnp.dot(repeat, slope1, preferred_element_type=F32).astype(BF16)
    slope_copies = [copy_to(kind, step, slopes.at[z_lo], slopes.at[z_lo]) for kind, step in OCTETS]
    pred_copies = [copy_to("z_hi", step, preds.at[z_hi], preds.at[z_hi]) for step in (1, 2, 3)]
    for k in range(4):
        for block in range(4):
            rows = slice(block * 256, block * 256 + 256)
            back[(z_hi - k + 4) % 4, block] = lax.dot_general(
                slope1, dense_w_ref[rows] if k == 0 else gathered[k - 1, rows], across,
                preferred_element_type=F32,
            )
    held_back = lax.dot_general(
        spread, back[...].reshape(256, 256), (((0,), (0,)), ((), ())), precision=EXACT,
        preferred_element_type=F32,
    )
    summed[...] = held_back.reshape(4, 64, 256)

    def turn(s, carry):
        spread_s = jnp.broadcast_to(summed[s].reshape(4, 1, 16, 256), (4, 4, 16, 256))
        cell = (spread_s.reshape(256, 256) * slope_at[s]).T.astype(BF16)
        for block in range(16):
            new = block % 2 * 8 + block // 2
            turned[s, new * 16 : new * 16 + 16] = cell[block * 16 : block * 16 + 16]
        return carry

    lax.fori_loop(0, 4, turn, 0)
    mine = pl.ds(pl.multiple_of(core * 128, 128), 128)
    theirs = pl.ds(pl.multiple_of(128 - core * 128, 128), 128)
    y_at = reserve(4)
    core_copies = []

    def y_copy(block, from_y):
        return pltpu.make_async_remote_copy(
            src_ref=y_out.at[block], dst_ref=y_in.at[from_y],
            send_sem=send_sem.at[y_at + block], recv_sem=recv_sem.at[y_at + from_y],
            device_id=partner("y", block - y + 4), device_id_type=MESH,
        )

    def over_y(block):
        core_copies[block].wait_recv()
        rows = slice(block * 864, block * 864 + 864)
        total = kern[rows, mine].astype(F32) + core_in[block].astype(F32)

        @pl.when(y == block)
        def _():
            y_sum[0:864] = total

        @pl.when(y != block)
        def _():
            y_out[block] = total.astype(BF16)
            y_copy(block, y).start()

    def grad_piece():
        for copy in feat_copies + slope_copies:
            copy.wait()
        return [copy_to("core", 1, feat, feat_pair), copy_to("core", 1, slopes, slopes_pair)]

    def grad_parts(pair):
        for copy in pair:
            copy.wait()
        over = (((0,), (0,)), ((), ()))
        slice_of = lax.broadcasted_iota(jnp.int32, (128, 128), 0) % 16 // 4

        def by_slice(ref):
            rows = ref[...].reshape(128, 128).astype(F32)
            return jnp.concatenate(
                [jnp.where(slice_of == d, rows, 0.0).astype(BF16) for d in range(4)], axis=1
            )

        grad = lax.dot_general(
            feat[...].reshape(128, 128), by_slice(slopes), over, preferred_element_type=F32
        ) + lax.dot_general(
            feat_pair[...].reshape(128, 128), by_slice(slopes_pair), over, preferred_element_type=F32
        )
        grad = jnp.where(core == 0, grad[0:64], grad[64:128])
        for d in range(4):
            part_out[d] = grad[:, d * 128 : d * 128 + 128].astype(BF16)
        return [
            copy_to("z_hi", step, part_out.at[(z_hi + step) % 4], part_in.at[step - 1])
            for step in (2, 1, 3)
        ]

    pair, part_copies = None, None
    for tap in range(9):
        a, b = tap // 3, tap % 3
        total = jnp.zeros((256, 384), F32)
        for s in range(4):
            total = total + jnp.dot(
                turned[s], wide[s, a : a + 4, b : b + 4].reshape(256, 384), preferred_element_type=F32
            )
        kern[tap * 384 : tap * 384 + 384] = total.T.astype(BF16)
        if tap in (2, 4, 6, 8):
            block = tap // 2 - 1
            rows = slice(block * 864, block * 864 + 864)
            core_copies.append(copy_to("core", 1, kern.at[rows, theirs], core_in.at[block]))
        if tap in (3, 5, 7):
            over_y(tap // 2 - 1)
        if tap == 7:
            pair = grad_piece()
    over_y(3)
    part_copies = grad_parts(pair)
    y_sum[864:896] = jnp.zeros((32, 128), F32)
    for block in range(4):

        @pl.when(y != block)
        def _(block=block):
            y_copy(block, block).wait()
            y_sum[0:864] = y_sum[0:864] + y_in[block].astype(F32)

    for hi in range(4):
        for to in range(4):
            start = (hi * 4 + to) * 54
            x_out[to, hi] = y_sum[start : start + 64].astype(BF16)
    x_copies = []
    for step in (1, 2, 3):
        x_copies.append(copy_to("x", step, x_out.at[(x + step) % 4], x_in.at[step - 1]))
    for copy in x_copies:
        copy.wait()
    blocks = (x_out[x].astype(F32) + x_in[0].astype(F32)) + (x_in[1].astype(F32) + x_in[2].astype(F32))
    for half in range(2):
        both = jnp.concatenate([blocks[2 * half].T, blocks[2 * half + 1].T], axis=1)
        lo_out[:, half] = both.reshape(8, 16, 128).astype(BF16)
    turn_copies = []
    for kind, step in OCTETS:
        turn_copies.append(copy_to(kind, step, lo_out.at[(z_lo + step) % 8], lo_in.at[step - 1]))
    for copy in turn_copies:
        copy.wait()
    total = lo_out[z_lo].astype(F32)
    for step in range(7):
        total = total + lo_in[step].astype(F32)
    hi_out[...] = total
    hi_copies = []
    for step in (2, 1, 3):
        hi_copies.append(copy_to("z_hi", step, hi_out.at[((z_hi + step) % 4) // 2], hi_in.at[step - 1]))
    for copy in part_copies:
        copy.wait()
    pieces[z_lo] = (
        (part_out[z_hi].astype(F32) + part_in[0].astype(F32))
        + (part_in[1].astype(F32) + part_in[2].astype(F32))
    ).astype(BF16)
    piece_copies = [copy_to(kind, step, pieces.at[z_lo], pieces.at[z_lo]) for kind, step in OCTETS]
    for copy in piece_copies:
        copy.wait()
    last = copy_to("core", 1, pieces, pieces_pair)
    for copy in pred_copies:
        copy.wait()
    pred_ref[...] = ((preds[0] + preds[1]) + (preds[2] + preds[3]))[:, 0:4]
    last.wait()
    for at in range(8):
        dense_ref[pl.ds(pl.multiple_of(at * 128 + core * 64, 64), 64)] = pieces[at].astype(F32)
        dense_ref[pl.ds(pl.multiple_of(at * 128 + 64 - core * 64, 64), 64)] = pieces_pair[at].astype(F32)
    for copy in hi_copies:
        copy.wait()
    total = (hi_out[z_hi // 2] + hi_in[0]) + (hi_in[1] + hi_in[2])
    across_rows = total.T
    conv_ref[...] = jnp.where(z_hi % 2 == 0, across_rows[0:54], across_rows[64:118])
    for copy in core_copies:
        copy.wait_send()


def per_device(volume, conv_weight, dense_weight, mid_weight, out_weight, targets):
    vmem = pl.BlockSpec(memory_space=pltpu.VMEM)
    predictions, dense_grad, conv_grad = pl.pallas_call(
        kernel,
        name="conv_and_head",
        out_shape=(
            jax.ShapeDtypeStruct((16, 4), F32),
            jax.ShapeDtypeStruct((1024, 128), F32),
            jax.ShapeDtypeStruct((54, 16), F32),
        ),
        in_specs=[vmem] * 6,
        out_specs=(vmem,) * 3,
        scratch_shapes=[
            pltpu.VMEM((4, 6, 6, 16, 128), BF16),
            pltpu.VMEM((4, 6, 6, 16, 384), BF16),
            pltpu.VMEM((4, 256, 256), F32),
            pltpu.VMEM((4, 64, 256), F32),
            pltpu.VMEM((4, 4, 16, 256), BF16),
            pltpu.VMEM((4, 16, 256), BF16),
            pltpu.VMEM((3, 1024, 128), BF16),
            pltpu.VMEM((2, 4, 16, 128), F32),
            pltpu.VMEM((4, 4, 16, 256), F32),
            pltpu.VMEM((4, 256, 256), BF16),
            pltpu.VMEM((4, 16, 128), F32),
            pltpu.VMEM((3456, 256), BF16),
            pltpu.VMEM((4, 864, 128), BF16),
            pltpu.VMEM((4, 864, 128), BF16),
            pltpu.VMEM((4, 864, 128), BF16),
            pltpu.VMEM((896, 128), F32),
            pltpu.VMEM((4, 4, 64, 128), BF16),
            pltpu.VMEM((3, 4, 64, 128), BF16),
            pltpu.VMEM((8, 2, 16, 128), BF16),
            pltpu.VMEM((7, 2, 16, 128), BF16),
            pltpu.VMEM((2, 16, 128), F32),
            pltpu.VMEM((3, 16, 128), F32),
            pltpu.VMEM((8, 16, 128), BF16),
            pltpu.VMEM((8, 16, 128), BF16),
            pltpu.VMEM((8, 16, 128), BF16),
            pltpu.VMEM((8, 16, 128), BF16),
            pltpu.VMEM((4, 64, 128), BF16),
            pltpu.VMEM((3, 64, 128), BF16),
            pltpu.VMEM((8, 64, 128), BF16),
            pltpu.VMEM((8, 64, 128), BF16),
            pltpu.SemaphoreType.DMA((COPIES,)),
            pltpu.SemaphoreType.DMA((COPIES,)),
            pltpu.SemaphoreType.DMA,
        ],
        compiler_params=pltpu.CompilerParams(
            collective_id=0, has_side_effects=True, vmem_limit_bytes=48 * 2**20
        ),
    )(
        volume.reshape(16, 4, 16, 128),
        conv_weight,
        dense_weight.reshape(1024, 128),
        mid_weight,
        out_weight,
        targets,
    )
    return predictions, dense_grad.reshape(dense_weight.shape), conv_grad


def solution(mesh):
    in_specs = (
        P("sample", "depth", "height", None, None),
        P(),
        P("depth", "height", None, None),
        P(),
        P(),
        P("sample", None),
    )
    out_specs = (
        P("sample", None),
        P("depth", "height", None, None),
        P(("depth", "height"), "sample"),
    )
    return jax.shard_map(
        per_device, mesh=mesh, in_specs=in_specs, out_specs=out_specs, check_vma=False
    )
```

time: 1810 us -> 144 us (0.08)
  waiting for transfers between devices: 1480 us -> 0 us
  blocking collectives: 272 us -> 0 us
  Pallas kernels: 0 us -> 133 us
  starting transfers between devices: 22.2 us -> 0 us
    unnamed x4 -> x0, waiting for transfers between devices: 1060 us -> none
    psum x1 -> x0, blocking collectives: 272 us -> none  [per_device(): first = lax.psum(partial_value, ('depth', 'height'))]
    psum x1 -> x0, waiting for transfers between devices: 234 us -> none  [per_device(): dense_grad = lax.psum(local_dense, 'sample').reshape(dense_weight.shape)]
    pallas_call x0 -> x1, Pallas kernels: none -> 133 us  [per_device(): pl.pallas_call(kernel, name='conv_and_head', out_shape=(jax.ShapeDtypeStr...]
    reduce_scatter x1 -> x0, waiting for transfers between devices: 124 us -> none  [per_device(): lax.psum_scatter(local_kernel, 'sample', scatter_dimension=1, tiled=True)]
    ppermute x4 -> x0, waiting for transfers between devices: 64.7 us -> none  [the longest x2 53.7 us: padded_2(): lax.ppermute(head, axis, [((i + 1) % count, i) for i in range(ends)])]
    ppermute x4 -> x0, starting transfers between devices: 22.1 us -> none  [the longest x2 19.5 us: padded_2(): lax.ppermute(tail, axis, [(i, (i + 1) % count) for i in range(ends)])]
  transfers between devices with their start and end apart: 7 -> 0, of which waited for: 7 -> 0; matrix products, arithmetic and copies ran while one was open for 0% -> 0% of each run, Pallas kernels for 0% -> 0%
where the time goes in v2:
time: 144 us; the launch traced here: 142 us
  Pallas kernels  133 us (92%)
  local copies, waits for them, and re-layouts  7.86 us (5%)
    pallas_call x1, Pallas kernels, per_device(): pl.pallas_call(kernel, name='conv_and_head', out_shape=(jax.ShapeDtypeStr...  133 us
    unnamed x12, local copies, waits for them, and re-layouts  7.86 us

profile of v2, /device:TPU:1, one launch (start us, length us, event | category | flops | bytes accessed | tf_op | source)
XLA Modules:
  0.0 141.9 jit_solution(4669554544614453136)
XLA Ops:
  0.6 0.8 copy.11.targets_ref
  1.4 0.8 copy.10.out_w_ref
  2.2 0.8 copy.9.mid_ref
  3.0 0.0 copy-start
  3.0 1.5 %copy-done = bf16[3456,256]{1,0:T(8,128)(2,1)S(1)} copy-done((bf16[3456,256]{1,0:T(8,128)(2,1)S(1)}, bf16[3456,256]{1,0:T(8,128)(2,1)}, u32[]{:S(2)}) %copy-start) | copy-done | bytes 1769496
  4.5 0.0 copy-start.1
  4.5 0.9 copy-done.1
  5.4 0.0 copy-start.2
  5.4 0.9 copy-done.2
  6.4 133.3 %conv_and_head.1 = (f32[16,4]{1,0:T(8,128)S(1)}, f32[1024,128]{1,0:T(8,128)S(1)}, f32[54,16]{1,0:T(8,128)S(1)}) custom-call(bf16[16,4,16,128]{3,2,1,0:T(8,128)(2,1)S(1)} %bitcast.4, bf16[3456,256]{1,0:T(8,128)(2,1)S(1)} %copy-done, bf16[1024,128]{1,0:T(8,128)(2,1)S(1)} %bitcast.5, f32[128,64]{1,0:T(8,128)S(1)} %copy.9.mid_ref, f32[64,4]{1,0:T(8,128)S(1)} %copy.10.out_w_ref, ...), custom_call_target="tpu_custom_call" | custom-call | tf_op jit(solution)/shard_map/conv_and_head/pallas_call | solution.py:399
  139.7 0.7 copy.12
  140.4 0.7 copy.13
  141.1 0.8 copy.15
Async XLA Ops:
  3.0 1.5 %copy-start = (bf16[3456,256]{1,0:T(8,128)(2,1)S(1)}, bf16[3456,256]{1,0:T(8,128)(2,1)}, u32[]{:S(2)}) copy-start(bf16[3456,256]{1,0:T(8,128)(2,1)} %weight_ref.1) | copy-start | bytes 5308420
  4.5 0.9 copy-start.1
  5.4 0.9 copy-start.2

commit v3 on v2

v3 whole, which is shorter than its diff:
```python
import jax
import jax.numpy as jnp
from jax import lax
from jax.experimental import pallas as pl
from jax.experimental.pallas import tpu as pltpu
from jax.sharding import PartitionSpec as P

F32 = jnp.float32
BF16 = jnp.bfloat16
MESH = pl.DeviceIdType.MESH
EXACT = lax.Precision.HIGHEST


def place():
    sample, depth, x = lax.axis_index("sample"), lax.axis_index("depth"), lax.axis_index("height")
    return sample // 2, sample % 2, depth // 4, depth % 4, x


def partner(kind, step):
    z_lo, core, y, z_hi, x = place()
    if kind == "z_lo":
        z_lo = (z_lo + step) % 8
    elif kind == "z_four":
        z_lo = (z_lo // 4) * 4 + (z_lo + step) % 4
    elif kind == "core":
        core = (core + step) % 2
    elif kind == "y":
        y = (y + step) % 4
    elif kind == "z_hi":
        z_hi = (z_hi + step) % 4
    elif kind == "x":
        x = (x + step) % 4
    else:
        y, x = (y + step[0]) % 4, (x + step[1]) % 4
    return (z_lo * 2 + core, y * 4 + z_hi, x)


QUADS = [(kind, step) for kind in ("x", "y", "z_hi") for step in (1, 2, 3)]
OTHERS = (2, 1, 3)
OCTET = range(1, 8)
CORNERS = [("corner", (dy, dx)) for dy in (1, 3) for dx in (1, 3)]
PARTNERS = [("core", 1)] + [q for q in QUADS if q != ("z_hi", 2)] + [("z_lo", step) for step in OCTET] + CORNERS
COPIES = 37


def gelu_and_slope(value):
    rate = 0.7978845608028654
    square = value * value
    bend = jnp.tanh(rate * (value + 0.044715 * value * square))
    half = 0.5 * (1.0 + bend)
    slope = half + 0.5 * value * (1.0 - bend * bend) * (rate * (1.0 + 3 * 0.044715 * square))
    return value * half, slope


def one_hot(shape, test, kind, weight=1.0):
    row = lax.broadcasted_iota(jnp.int32, shape, 0)
    column = lax.broadcasted_iota(jnp.int32, shape, 1)
    return jnp.where(test(row, column), weight, 0.0).astype(kind)


def kernel(
    vol_ref, weight_hbm, dense_w_hbm, mid_hbm, out_w_hbm, targets_hbm,
    pred_ref, dense_ref, conv_ref,
    weight_ref, dense_w_ref, mid_ref, out_w_ref, targets_ref,
    ext, wide, slope_at, summed, pool, pool_out, pool_in, vol_relay, gathered, held, back, turned, preds,
    kern, core_in, y_out, y_in, y_sum, x_out, x_in, lo_out, lo_in, hi_out, hi_in,
    feat, slopes, slope_in,
    send_sem, recv_sem, local_sem,
):
    z_lo, core, y, z_hi, x = place()
    used = [0]

    def reserve(count):
        used[0] += count
        assert used[0] <= COPIES
        return used[0] - count

    def copy_to(kind, step, src, dst):
        at = reserve(1)
        copy = pltpu.make_async_remote_copy(
            src_ref=src, dst_ref=dst, send_sem=send_sem.at[at], recv_sem=recv_sem.at[at],
            device_id=partner(kind, step), device_id_type=MESH,
        )
        copy.start()
        return copy

    def group_to(kind, steps, pair_of, span):
        at = reserve(1)
        sems = dict(send_sem=send_sem.at[at], recv_sem=recv_sem.at[at], device_id_type=MESH)
        for step in steps:
            src, dst = pair_of(step)
            pltpu.make_async_remote_copy(
                src_ref=src, dst_ref=dst, device_id=partner(kind, step), **sems
            ).start()
        return pltpu.make_async_remote_copy(
            src_ref=span, dst_ref=span, device_id=partner(kind, steps[0]), **sems
        )

    barrier = pltpu.get_barrier_semaphore()
    for kind, step in PARTNERS:
        pl.semaphore_signal(barrier, inc=1, device_id=partner(kind, step), device_id_type=MESH)
    local = [
        (vol_ref.at[pl.ds(z_hi * 4, 4)], ext.at[:, 1 + z_hi, 1:5]),
        (dense_w_hbm, dense_w_ref),
        (weight_hbm, weight_ref),
        (mid_hbm, mid_ref),
        (out_w_hbm, out_w_ref),
        (targets_hbm, targets_ref),
    ]
    local = [pltpu.make_async_copy(src, dst, local_sem.at[at]) for at, (src, dst) in enumerate(local)]
    for copy in local:
        copy.start()
    pl.semaphore_wait(barrier, len(PARTNERS))

    far = (z_hi + 2) % 4
    ways = ((0, 1), (1, 3))
    vol_on = [
        copy_to("z_hi", step, vol_ref.at[pl.ds(far * 4 + 2 * way, 2)], vol_relay.at[way])
        for way, step in ways
    ]
    vol_copies = [
        copy_to("z_hi", step, vol_ref.at[pl.ds((z_hi + step) % 4 * 4, 4)], ext.at[:, 1 + z_hi, 1:5])
        for way, step in ways
    ]
    start = pl.multiple_of(core * 512 + (z_lo % 4) * 128, 128)
    share = pl.ds(start, 128)
    for (way, step), copy in zip(ways, vol_on):
        copy.wait_recv()
        vol_copies.append(
            copy_to(
                "z_hi", step, vol_relay.at[way],
                ext.at[2 * way : 2 * way + 2, 1 + (z_hi + 4 - step) % 4, 1:5],
            )
        )
    hi_weights = group_to(
        "z_hi", OTHERS,
        lambda step: (dense_w_hbm.at[share], gathered.at[step - 1, share]),
        gathered.at[:, share],
    )
    for copy in local:
        copy.wait()
    for copy in vol_copies:
        copy.wait_recv()
    y_halo = [
        copy_to("y", 1, ext.at[:, 4, 1:5], ext.at[:, 0, 1:5]),
        copy_to("y", 3, ext.at[:, 1, 1:5], ext.at[:, 5, 1:5]),
    ]
    x_halo = [
        copy_to("x", 1, ext.at[:, 1:5, 4], ext.at[:, 1:5, 0]),
        copy_to("x", 3, ext.at[:, 1:5, 1], ext.at[:, 1:5, 5]),
    ]
    for kind, (dy, dx) in CORNERS:
        src = ext.at[:, 4 if dy == 1 else 1, 4 if dx == 1 else 1]
        dst = ext.at[:, 0 if dy == 1 else 5, 0 if dx == 1 else 5]
        x_halo.append(copy_to(kind, (dy, dx), src, dst))
    hi_weights.wait()
    lo_weights = group_to(
        "z_four", (1, 2, 3),
        lambda step: (gathered.at[:, share], gathered.at[:, share]),
        gathered.at[:, 0:384],
    )
    for copy in x_halo + y_halo:
        copy.wait()
    for copy in vol_on + vol_copies:
        copy.wait_send()

    @pl.when(y == 0)
    def _():
        ext[:, 0] = jnp.zeros((4, 6, 16, 128), BF16)

    @pl.when(y == 3)
    def _():
        ext[:, 5] = jnp.zeros((4, 6, 16, 128), BF16)

    @pl.when(x == 0)
    def _():
        ext[:, :, 0] = jnp.zeros((4, 6, 16, 128), BF16)

    @pl.when(x == 3)
    def _():
        ext[:, :, 5] = jnp.zeros((4, 6, 16, 128), BF16)

    def forward(s, carry):
        cells = ext[s].reshape(36, 16, 128).astype(F32)
        edge = jnp.zeros((36, 1, 128), F32)
        wide[s, :, :, :, 0:128] = (
            jnp.concatenate([edge, cells[:, :15]], axis=1).astype(BF16).reshape(6, 6, 16, 128)
        )
        wide[s, :, :, :, 128:256] = ext[s]
        wide[s, :, :, :, 256:384] = (
            jnp.concatenate([cells[:, 1:], edge], axis=1).astype(BF16).reshape(6, 6, 16, 128)
        )
        pre = jnp.zeros((256, 256), F32)
        for tap in range(9):
            a, b = tap // 3, tap % 3
            pre = pre + jnp.dot(
                wide[s, a : a + 4, b : b + 4].reshape(256, 384),
                weight_ref[tap * 384 : tap * 384 + 384],
                preferred_element_type=F32,
            )
        active, slope = gelu_and_slope(pre)
        slope_at[s] = slope
        summed[s] = jnp.sum(active.reshape(4, 4, 16, 256), axis=1).reshape(64, 256)
        return carry

    lax.fori_loop(0, 4, forward, 0)
    lo_weights.wait()
    half_rows = pl.ds(pl.multiple_of(core * 512, 512), 512)
    pair_weights = copy_to("core", 1, gathered.at[:, half_rows], gathered.at[:, half_rows])

    spread = one_hot(
        (256, 256),
        lambda r, c: (r // 64 == c // 16 % 4)
        & (r // 16 % 4 == c % 16 // 4)
        & (r % 16 == z_hi * 4 + c // 64),
        F32,
        1.0 / 16,
    )
    pooled = jnp.dot(
        spread, summed[...].reshape(256, 256), precision=EXACT, preferred_element_type=F32
    ).astype(BF16)
    pool[...] = pooled.reshape(4, 4, 16, 256)
    order = one_hot(
        (64, 256),
        lambda r, c: (r // 16 == c // 64)
        & (r // 4 % 4 == c // 16 % 4)
        & (z_hi * 4 + r % 4 == c % 16),
        BF16,
    )
    pool_out[...] = (
        jnp.dot(order, pooled, preferred_element_type=F32).astype(BF16).reshape(4, 16, 256)
    )
    pool_in[z_hi] = pool_out[z_hi]
    pool_copies = group_to(
        "z_hi", OTHERS,
        lambda step: (pool_out.at[(z_hi + step) % 4], pool_in.at[z_hi]),
        pool_in.at[0:3],
    )
    total = jnp.zeros((16, 128), F32)
    for k in range(4):
        if k == 1:
            pair_weights.wait()
        for block in range(4):
            rows = slice(block * 256, block * 256 + 256)
            total = total + jnp.dot(
                pool[(z_hi - k + 4) % 4, block],
                dense_w_ref[rows] if k == 0 else gathered[k - 1, rows],
                preferred_element_type=F32,
            )
    for stage, (kind, mine) in enumerate((("x", x), ("y", y))):
        held[stage, mine] = total
        group_to(
            kind, OTHERS,
            lambda step: (held.at[stage, mine], held.at[stage, mine]),
            held.at[stage, 0:3],
        ).wait()
        total = (held[stage, 0] + held[stage, 1]) + (held[stage, 2] + held[stage, 3])
    first = total
    out_w = jnp.concatenate([out_w_ref[...], jnp.zeros((124, 64), F32)], axis=0)
    across = (((1,), (1,)), ((), ()))
    targets = lax.dot_general(
        one_hot((16, 16), lambda r, c: r == c, F32),
        jnp.concatenate([targets_ref[...], jnp.zeros((124, 16), F32)], axis=0),
        across, precision=EXACT, preferred_element_type=F32,
    )
    first_gelu, first_slope = gelu_and_slope(first)
    second = lax.dot_general(
        first_gelu, mid_ref[...], across, precision=EXACT, preferred_element_type=F32
    )
    second_gelu, second_slope = gelu_and_slope(second)
    pred = lax.dot_general(second_gelu, out_w, across, precision=EXACT, preferred_element_type=F32)
    slope2 = second_slope * jnp.dot(
        pred - targets, out_w, precision=EXACT, preferred_element_type=F32
    )
    slope1 = first_slope * jnp.dot(
        slope2, mid_ref[...], precision=EXACT, preferred_element_type=F32
    )
    ours = lax.broadcasted_iota(jnp.int32, (16, 128), 0) // 4 == z_hi
    slope1 = jnp.where(ours, slope1, 0.0).astype(BF16)
    preds[z_hi] = jnp.where(ours, pred, 0.0)
    slope_in[z_hi] = slope1
    slope_copies = group_to(
        "z_hi", OTHERS, lambda step: (slope_in.at[z_hi], slope_in.at[z_hi]), slope_in.at[0:3]
    )
    pred_copies = group_to(
        "z_hi", OTHERS, lambda step: (preds.at[z_hi], preds.at[z_hi]), preds.at[0:3]
    )
    for k in range(4):
        for block in range(4):
            rows = slice(block * 256, block * 256 + 256)
            back[(z_hi - k + 4) % 4, block] = lax.dot_general(
                slope1, dense_w_ref[rows] if k == 0 else gathered[k - 1, rows], across,
                preferred_element_type=F32,
            )
    held_back = lax.dot_general(
        spread, back[...].reshape(256, 256), (((0,), (0,)), ((), ())), precision=EXACT,
        preferred_element_type=F32,
    )
    summed[...] = held_back.reshape(4, 64, 256)

    def turn(s, carry):
        spread_s = jnp.broadcast_to(summed[s].reshape(4, 1, 16, 256), (4, 4, 16, 256))
        cell = (spread_s.reshape(256, 256) * slope_at[s]).T.astype(BF16)
        for block in range(16):
            new = block % 2 * 8 + block // 2
            turned[s, new * 16 : new * 16 + 16] = cell[block * 16 : block * 16 + 16]
        return carry

    lax.fori_loop(0, 4, turn, 0)
    mine = pl.ds(pl.multiple_of(core * 128, 128), 128)
    theirs = pl.ds(pl.multiple_of(128 - core * 128, 128), 128)
    y_at = reserve(4)
    core_copies = []

    def y_copy(block, from_y):
        return pltpu.make_async_remote_copy(
            src_ref=y_out.at[block], dst_ref=y_in.at[from_y],
            send_sem=send_sem.at[y_at + block], recv_sem=recv_sem.at[y_at + from_y],
            device_id=partner("y", block - y + 4), device_id_type=MESH,
        )

    def over_y(block):
        core_copies[block].wait_recv()
        rows = slice(block * 864, block * 864 + 864)
        total = kern[rows, mine].astype(F32) + core_in[block].astype(F32)

        @pl.when(y == block)
        def _():
            y_sum[0:864] = total

        @pl.when(y != block)
        def _():
            y_out[block] = total.astype(BF16)
            y_copy(block, y).start()

    def hand_pooled():
        pool_copies.wait()
        order = one_hot(
            (64, 64),
            lambda r, c: (r // 16 == c // 4 % 4) & (r % 16 == c // 16 * 4 + c % 4),
            BF16,
        )
        rows = jnp.dot(order, pool_in[...].reshape(64, 256), preferred_element_type=F32)
        feat[core, z_lo] = rows.astype(BF16).reshape(4, 16, 256)
        return group_to(
            "z_lo", OCTET, lambda step: (feat.at[core, z_lo], feat.at[core, z_lo]), feat.at[core, 0:7]
        )

    def hand_slopes():
        slope_copies.wait()
        rows = (slope_in[0].astype(F32) + slope_in[1].astype(F32)) + (
            slope_in[2].astype(F32) + slope_in[3].astype(F32)
        )
        slopes[core, z_lo] = rows.astype(BF16)
        return group_to(
            "z_lo", OCTET,
            lambda step: (slopes.at[core, z_lo], slopes.at[core, z_lo]),
            slopes.at[core, 0:7],
        )

    for tap in range(9):
        a, b = tap // 3, tap % 3
        total = jnp.zeros((256, 384), F32)
        for s in range(4):
            total = total + jnp.dot(
                turned[s], wide[s, a : a + 4, b : b + 4].reshape(256, 384), preferred_element_type=F32
            )
        kern[tap * 384 : tap * 384 + 384] = total.T.astype(BF16)
        if tap in (2, 4, 6, 8):
            block = tap // 2 - 1
            rows = slice(block * 864, block * 864 + 864)
            core_copies.append(copy_to("core", 1, kern.at[rows, theirs], core_in.at[block]))
        if tap in (3, 5, 7):
            over_y(tap // 2 - 1)
        if tap == 5:
            feat_copies = hand_pooled()
    over_y(3)
    lo_slopes = hand_slopes()
    y_sum[864:896] = jnp.zeros((32, 128), F32)
    for block in range(4):

        @pl.when(y != block)
        def _(block=block):
            y_copy(block, block).wait()
            y_sum[0:864] = y_sum[0:864] + y_in[block].astype(F32)

    for hi in range(4):
        for to in range(4):
            start = (hi * 4 + to) * 54
            x_out[to, hi] = y_sum[start : start + 64].astype(BF16)
    group_to(
        "x", OTHERS, lambda step: (x_out.at[(x + step) % 4], x_in.at[step - 1]), x_in.at[0:3]
    ).wait()
    blocks = (x_out[x].astype(F32) + x_in[0].astype(F32)) + (x_in[1].astype(F32) + x_in[2].astype(F32))
    for half in range(2):
        both = jnp.concatenate([blocks[2 * half].T, blocks[2 * half + 1].T], axis=1)
        lo_out[:, half] = both.reshape(8, 16, 128).astype(BF16)
    turn_copies = group_to(
        "z_lo", OCTET, lambda step: (lo_out.at[(z_lo + step) % 8], lo_in.at[step - 1]), lo_in.at[0:7]
    )
    feat_copies.wait()
    lo_slopes.wait()
    pair = [
        copy_to("core", 1, feat.at[core], feat.at[core]),
        copy_to("core", 1, slopes.at[core], slopes.at[core]),
    ]
    turn_copies.wait()
    total = lo_out[z_lo].astype(F32)
    for step in range(7):
        total = total + lo_in[step].astype(F32)
    hi_out[...] = total
    hi_copies = group_to(
        "z_hi", OTHERS,
        lambda step: (hi_out.at[((z_hi + step) % 4) // 2], hi_in.at[step - 1]),
        hi_in.at[0:3],
    )
    for copy in pair:
        copy.wait()
    over = (((0,), (0,)), ((), ()))
    for block in range(4):
        sums = [
            lax.dot_general(
                feat[c, :, block].reshape(128, 256), slopes[c].reshape(128, 128), over,
                preferred_element_type=F32,
            )
            for c in range(2)
        ]
        dense_ref[block * 256 : block * 256 + 256] = sums[0] + sums[1]
    pred_copies.wait()
    sums = (preds[0] + preds[1]) + (preds[2] + preds[3])
    pred_ref[...] = jnp.concatenate([sums, jnp.zeros((112, 128), F32)], axis=0).T[0:4, 0:16]
    hi_copies.wait()
    total = (hi_out[z_hi // 2] + hi_in[0]) + (hi_in[1] + hi_in[2])
    conv_ref[...] = jnp.where(z_hi % 2 == 0, total[:, 0:54], total[:, 64:118])
    for copy in core_copies:
        copy.wait_send()
    assert used[0] == COPIES


def per_device(volume, conv_weight, dense_weight, mid_weight, out_weight, targets):
    vmem = pl.BlockSpec(memory_space=pltpu.VMEM)
    hbm = pl.BlockSpec(memory_space=pltpu.HBM)
    predictions, dense_grad, conv_grad = pl.pallas_call(
        kernel,
        name="conv_and_head",
        out_shape=(
            jax.ShapeDtypeStruct((4, 16), F32),
            jax.ShapeDtypeStruct((1024, 128), F32),
            jax.ShapeDtypeStruct((16, 54), F32),
        ),
        in_specs=[hbm] * 6,
        out_specs=(vmem,) * 3,
        scratch_shapes=[
            pltpu.VMEM((3456, 256), BF16),
            pltpu.VMEM((1024, 128), BF16),
            pltpu.VMEM((64, 128), F32),
            pltpu.VMEM((4, 64), F32),
            pltpu.VMEM((4, 16), F32),
            pltpu.VMEM((4, 6, 6, 16, 128), BF16),
            pltpu.VMEM((4, 6, 6, 16, 384), BF16),
            pltpu.VMEM((4, 256, 256), F32),
            pltpu.VMEM((4, 64, 256), F32),
            pltpu.VMEM((4, 4, 16, 256), BF16),
            pltpu.VMEM((4, 16, 256), BF16),
            pltpu.VMEM((4, 16, 256), BF16),
            pltpu.VMEM((2, 2, 4, 16, 128), BF16),
            pltpu.VMEM((3, 1024, 128), BF16),
            pltpu.VMEM((2, 4, 16, 128), F32),
            pltpu.VMEM((4, 4, 16, 256), F32),
            pltpu.VMEM((4, 256, 256), BF16),
            pltpu.VMEM((4, 16, 128), F32),
            pltpu.VMEM((3456, 256), BF16),
            pltpu.VMEM((4, 864, 128), BF16),
            pltpu.VMEM((4, 864, 128), BF16),
            pltpu.VMEM((4, 864, 128), BF16),
            pltpu.VMEM((896, 128), F32),
            pltpu.VMEM((4, 4, 64, 128), BF16),
            pltpu.VMEM((3, 4, 64, 128), BF16),
            pltpu.VMEM((8, 2, 16, 128), BF16),
            pltpu.VMEM((7, 2, 16, 128), BF16),
            pltpu.VMEM((2, 16, 128), F32),
            pltpu.VMEM((3, 16, 128), F32),
            pltpu.VMEM((2, 8, 4, 16, 256), BF16),
            pltpu.VMEM((2, 8, 16, 128), BF16),
            pltpu.VMEM((4, 16, 128), BF16),
            pltpu.SemaphoreType.DMA((COPIES,)),
            pltpu.SemaphoreType.DMA((COPIES,)),
            pltpu.SemaphoreType.DMA((6,)),
        ],
        compiler_params=pltpu.CompilerParams(
            collective_id=0, has_side_effects=True, vmem_limit_bytes=40 * 2**20
        ),
    )(
        *(
            pltpu.with_memory_space_constraint(array, pltpu.HBM)
            for array in (
                volume.reshape(16, 4, 16, 128),
                conv_weight,
                dense_weight.reshape(1024, 128),
                mid_weight.T,
                out_weight.T,
                targets.T,
            )
        )
    )
    return predictions.T, dense_grad.reshape(dense_weight.shape), conv_grad.T


def solution(mesh):
    in_specs = (
        P("sample", "depth", "height", None, None),
        P(),
        P("depth", "height", None, None),
        P(),
        P(),
        P("sample", None),
    )
    out_specs = (
        P("sample", None),
        P("depth", "height", None, None),
        P(("depth", "height"), "sample"),
    )
    return jax.shard_map(
        per_device, mesh=mesh, in_specs=in_specs, out_specs=out_specs, check_vma=False
    )
```

time: 144 us -> 131 us (0.910)
  Pallas kernels: 133 us -> 127 us
  local copies, waits for them, and re-layouts: 7.86 us -> 1.97 us
    pallas_call x1, Pallas kernels: 133 us -> 127 us  [per_device(): pl.pallas_call(kernel, name='conv_and_head', out_shape=(jax.ShapeDtypeStr...]
    unnamed x12 -> x3, local copies, waits for them, and re-layouts: 7.86 us -> 1.97 us
where the time goes in v3:
time: 131 us; the launch traced here: 129 us
  Pallas kernels  127 us (97%)
  local copies, waits for them, and re-layouts  1.97 us (2%)
    pallas_call x1, Pallas kernels, per_device(): pl.pallas_call(kernel, name='conv_and_head', out_shape=(jax.ShapeDtypeStr...  127 us

profile of v3, /device:TPU:1, one launch (start us, length us, event | category | flops | bytes accessed | tf_op | source)
XLA Modules:
  0.0 129.2 jit_solution(11180116295647534095)
XLA Ops:
  0.6 126.6 %conv_and_head.1 = (f32[4,16]{1,0:T(4,128)S(1)}, f32[1024,128]{1,0:T(8,128)S(1)}, f32[16,54]{1,0:T(8,128)S(1)}) custom-call(bf16[16,4,16,128]{3,2,1,0:T(8,128)(2,1)} %bitcast.11, bf16[3456,256]{1,0:T(8,128)(2,1)} %weight_hbm.1, bf16[1024,128]{1,0:T(8,128)(2,1)} %bitcast.12, f32[64,128]{1,0:T(8,128)} %bitcast.13, f32[4,64]{1,0:T(4,128)} %bitcast.14, ...), custom_call_target="tpu_custom_call" | custom-call | tf_op jit(solution)/shard_map/conv_and_head/pallas_call | solution.py:443
  127.2 0.6 copy.12
  127.8 0.8 copy.13
  128.6 0.6 copy.14

commit v4 on v3

--- a/solution.py
+++ b/solution.py
@@ -40,7 +40,7 @@
 OCTET = range(1, 8)
 CORNERS = [("corner", (dy, dx)) for dy in (1, 3) for dx in (1, 3)]
 PARTNERS = [("core", 1)] + [q for q in QUADS if q != ("z_hi", 2)] + [("z_lo", step) for step in OCTET] + CORNERS
-COPIES = 37
+COPIES = 42
 
 
 def gelu_and_slope(value):
@@ -63,7 +63,8 @@
     pred_ref, dense_ref, conv_ref,
     weight_ref, dense_w_ref, mid_ref, out_w_ref, targets_ref,
     ext, wide, slope_at, summed, pool, pool_out, pool_in, vol_relay, gathered, held, back, turned, preds,
-    kern, core_in, y_out, y_in, y_sum, x_out, x_in, lo_out, lo_in, hi_out, hi_in,
+    kern, core_in, y_out, y_in, y_sum, x_out, x_in,
+    lower, x_first, x_first_in, y_last, y_last_in, lo_out, lo_in, hi_out, hi_in,
     feat, slopes, slope_in,
     send_sem, recv_sem, local_sem,
 ):
@@ -310,7 +311,8 @@
     mine = pl.ds(pl.multiple_of(core * 128, 128), 128)
     theirs = pl.ds(pl.multiple_of(128 - core * 128, 128), 128)
     y_at = reserve(4)
-    core_copies = []
+    core_copies, x_first_copies = [], []
+    lower[432:448] = jnp.zeros((16, 128), F32)
 
     def y_copy(block, from_y):
         return pltpu.make_async_remote_copy(
@@ -326,12 +328,25 @@
 
         @pl.when(y == block)
         def _():
-            y_sum[0:864] = total
+            y_sum[0:432] = total[0:432]
 
         @pl.when(y != block)
         def _():
-            y_out[block] = total.astype(BF16)
+            y_out[block] = total[0:432].astype(BF16)
             y_copy(block, y).start()
+
+        lower[0:432] = total[432:864]
+        for hi in range(2):
+            for to in range(4):
+                start = (hi * 4 + to) * 54
+                x_first[to, block, hi] = lower[start : start + 64].astype(BF16)
+        x_first_copies.append(
+            group_to(
+                "x", OTHERS,
+                lambda step: (x_first.at[(x + step) % 4, block], x_first_in.at[block, step - 1]),
+                x_first_in.at[block],
+            )
+        )
 
     def hand_pooled():
         pool_copies.wait()
@@ -376,24 +391,42 @@
             feat_copies = hand_pooled()
     over_y(3)
     lo_slopes = hand_slopes()
-    y_sum[864:896] = jnp.zeros((32, 128), F32)
+    y_sum[432:448] = jnp.zeros((16, 128), F32)
     for block in range(4):
 
         @pl.when(y != block)
         def _(block=block):
             y_copy(block, block).wait()
-            y_sum[0:864] = y_sum[0:864] + y_in[block].astype(F32)
-
-    for hi in range(4):
+            y_sum[0:432] = y_sum[0:432] + y_in[block].astype(F32)
+
+    for hi in range(2):
         for to in range(4):
             start = (hi * 4 + to) * 54
             x_out[to, hi] = y_sum[start : start + 64].astype(BF16)
-    group_to(
+    x_copies = group_to(
         "x", OTHERS, lambda step: (x_out.at[(x + step) % 4], x_in.at[step - 1]), x_in.at[0:3]
-    ).wait()
-    blocks = (x_out[x].astype(F32) + x_in[0].astype(F32)) + (x_in[1].astype(F32) + x_in[2].astype(F32))
-    for half in range(2):
-        both = jnp.concatenate([blocks[2 * half].T, blocks[2 * half + 1].T], axis=1)
+    )
+    for block in range(4):
+        x_first_copies[block].wait()
+        y_last[block] = (
+            (x_first[x, block].astype(F32) + x_first_in[block, 0].astype(F32))
+            + (x_first_in[block, 1].astype(F32) + x_first_in[block, 2].astype(F32))
+        ).astype(BF16)
+    y_last_copies = group_to(
+        "y", OTHERS,
+        lambda step: (y_last.at[(y + step) % 4], y_last_in.at[step - 1]),
+        y_last_in.at[0:3],
+    )
+    x_copies.wait()
+    upper_blocks = (x_out[x].astype(F32) + x_in[0].astype(F32)) + (
+        x_in[1].astype(F32) + x_in[2].astype(F32)
+    )
+    y_last_copies.wait()
+    lower_blocks = (y_last[y].astype(F32) + y_last_in[0].astype(F32)) + (
+        y_last_in[1].astype(F32) + y_last_in[2].astype(F32)
+    )
+    for half, blocks in enumerate((upper_blocks, lower_blocks)):
+        both = jnp.concatenate([blocks[0].T, blocks[1].T], axis=1)
         lo_out[:, half] = both.reshape(8, 16, 128).astype(BF16)
     turn_copies = group_to(
         "z_lo", OCTET, lambda step: (lo_out.at[(z_lo + step) % 8], lo_in.at[step - 1]), lo_in.at[0:7]
@@ -408,10 +441,12 @@
     total = lo_out[z_lo].astype(F32)
     for step in range(7):
         total = total + lo_in[step].astype(F32)
-    hi_out[...] = total
+    for hi in range(4):
+        lanes = slice(hi % 2 * 64, hi % 2 * 64 + 64)
+        hi_out[hi] = jnp.concatenate([total[hi // 2, 0:8, lanes], total[hi // 2, 8:16, lanes]], axis=1)
     hi_copies = group_to(
         "z_hi", OTHERS,
-        lambda step: (hi_out.at[((z_hi + step) % 4) // 2], hi_in.at[step - 1]),
+        lambda step: (hi_out.at[(z_hi + step) % 4], hi_in.at[step - 1]),
         hi_in.at[0:3],
     )
     for copy in pair:
@@ -430,8 +465,9 @@
     sums = (preds[0] + preds[1]) + (preds[2] + preds[3])
     pred_ref[...] = jnp.concatenate([sums, jnp.zeros((112, 128), F32)], axis=0).T[0:4, 0:16]
     hi_copies.wait()
-    total = (hi_out[z_hi // 2] + hi_in[0]) + (hi_in[1] + hi_in[2])
-    conv_ref[...] = jnp.where(z_hi % 2 == 0, total[:, 0:54], total[:, 64:118])
+    total = (hi_out[z_hi] + hi_in[0]) + (hi_in[1] + hi_in[2])
+    conv_ref[0:8] = total[:, 0:54]
+    conv_ref[8:16] = total[:, 64:118]
     for copy in core_copies:
         copy.wait_send()
     assert used[0] == COPIES
@@ -471,15 +507,20 @@
             pltpu.VMEM((4, 16, 128), F32),
             pltpu.VMEM((3456, 256), BF16),
             pltpu.VMEM((4, 864, 128), BF16),
-            pltpu.VMEM((4, 864, 128), BF16),
-            pltpu.VMEM((4, 864, 128), BF16),
-            pltpu.VMEM((896, 128), F32),
-            pltpu.VMEM((4, 4, 64, 128), BF16),
-            pltpu.VMEM((3, 4, 64, 128), BF16),
+            pltpu.VMEM((4, 432, 128), BF16),
+            pltpu.VMEM((4, 432, 128), BF16),
+            pltpu.VMEM((448, 128), F32),
+            pltpu.VMEM((4, 2, 64, 128), BF16),
+            pltpu.VMEM((3, 2, 64, 128), BF16),
+            pltpu.VMEM((448, 128), F32),
+            pltpu.VMEM((4, 4, 2, 64, 128), BF16),
+            pltpu.VMEM((4, 3, 2, 64, 128), BF16),
+            pltpu.VMEM((4, 2, 64, 128), BF16),
+            pltpu.VMEM((3, 2, 64, 128), BF16),
             pltpu.VMEM((8, 2, 16, 128), BF16),
             pltpu.VMEM((7, 2, 16, 128), BF16),
-            pltpu.VMEM((2, 16, 128), F32),
-            pltpu.VMEM((3, 16, 128), F32),
+            pltpu.VMEM((4, 8, 128), F32),
+            pltpu.VMEM((3, 8, 128), F32),
             pltpu.VMEM((2, 8, 4, 16, 256), BF16),
             pltpu.VMEM((2, 8, 16, 128), BF16),
             pltpu.VMEM((4, 16, 128), BF16),

time: 131 us -> 127 us (0.969)
  Pallas kernels: 127 us -> 123 us
    pallas_call x1, Pallas kernels: 127 us -> 123 us  [per_device(): pl.pallas_call(kernel, name='conv_and_head', out_shape=(jax.ShapeDtypeStr...]
where the time goes in v4:
time: 127 us; the launch traced here: 126 us
  Pallas kernels  123 us (97%)
  local copies, waits for them, and re-layouts  1.97 us (2%)
    pallas_call x1, Pallas kernels, per_device(): pl.pallas_call(kernel, name='conv_and_head', out_shape=(jax.ShapeDtypeStr...  123 us

profile of v4, /device:TPU:1, one launch (start us, length us, event | category | flops | bytes accessed | tf_op | source)
XLA Modules:
  0.0 125.8 jit_solution(3515199231958047048)
XLA Ops:
  0.6 123.2 %conv_and_head.1 = (f32[4,16]{1,0:T(4,128)S(1)}, f32[1024,128]{1,0:T(8,128)S(1)}, f32[16,54]{1,0:T(8,128)S(1)}) custom-call(bf16[16,4,16,128]{3,2,1,0:T(8,128)(2,1)} %bitcast.11, bf16[3456,256]{1,0:T(8,128)(2,1)} %weight_hbm.1, bf16[1024,128]{1,0:T(8,128)(2,1)} %bitcast.12, f32[64,128]{1,0:T(8,128)} %bitcast.13, f32[4,64]{1,0:T(4,128)} %bitcast.14, ...), custom_call_target="tpu_custom_call" | custom-call | tf_op jit(solution)/shard_map/conv_and_head/pallas_call | solution.py:479
  123.8 0.6 copy.12
  124.4 0.8 copy.13
  125.2 0.6 copy.14

commit v5 on v4

--- a/solution.py
+++ b/solution.py
@@ -35,12 +35,12 @@
     return (z_lo * 2 + core, y * 4 + z_hi, x)
 
 
-QUADS = [(kind, step) for kind in ("x", "y", "z_hi") for step in (1, 2, 3)]
+AROUND = [(dy, dx) for dy in (2, 1, 3, 0) for dx in (2, 1, 3, 0) if (dy, dx) != (0, 0)]
 OTHERS = (2, 1, 3)
 OCTET = range(1, 8)
 CORNERS = [("corner", (dy, dx)) for dy in (1, 3) for dx in (1, 3)]
-PARTNERS = [("core", 1)] + [q for q in QUADS if q != ("z_hi", 2)] + [("z_lo", step) for step in OCTET] + CORNERS
-COPIES = 42
+PARTNERS = [("core", 1)] + [("z_hi", 1), ("z_hi", 3)] + [("z_lo", step) for step in OCTET] + [("corner", step) for step in AROUND]
+COPIES = 41
 
 
 def gelu_and_slope(value):
@@ -248,14 +248,12 @@
                 dense_w_ref[rows] if k == 0 else gathered[k - 1, rows],
                 preferred_element_type=F32,
             )
-    for stage, (kind, mine) in enumerate((("x", x), ("y", y))):
-        held[stage, mine] = total
-        group_to(
-            kind, OTHERS,
-            lambda step: (held.at[stage, mine], held.at[stage, mine]),
-            held.at[stage, 0:3],
-        ).wait()
-        total = (held[stage, 0] + held[stage, 1]) + (held[stage, 2] + held[stage, 3])
+    here = y * 4 + x
+    held[here] = total
+    group_to("corner", AROUND, lambda step: (held.at[here], held.at[here]), held.at[0:15]).wait()
+    total = held[0]
+    for at in range(1, 16):
+        total = total + held[at]
     first = total
     out_w = jnp.concatenate([out_w_ref[...], jnp.zeros((124, 64), F32)], axis=0)
     across = (((1,), (1,)), ((), ()))
@@ -390,7 +388,6 @@
         if tap == 5:
             feat_copies = hand_pooled()
     over_y(3)
-    lo_slopes = hand_slopes()
     y_sum[432:448] = jnp.zeros((16, 128), F32)
     for block in range(4):
 
@@ -406,6 +403,7 @@
     x_copies = group_to(
         "x", OTHERS, lambda step: (x_out.at[(x + step) % 4], x_in.at[step - 1]), x_in.at[0:3]
     )
+    lo_slopes = hand_slopes()
     for block in range(4):
         x_first_copies[block].wait()
         y_last[block] = (
@@ -501,7 +499,7 @@
             pltpu.VMEM((4, 16, 256), BF16),
             pltpu.VMEM((2, 2, 4, 16, 128), BF16),
             pltpu.VMEM((3, 1024, 128), BF16),
-            pltpu.VMEM((2, 4, 16, 128), F32),
+            pltpu.VMEM((16, 16, 128), F32),
             pltpu.VMEM((4, 4, 16, 256), F32),
             pltpu.VMEM((4, 256, 256), BF16),
             pltpu.VMEM((4, 16, 128), F32),

time: 127 us -> 125 us (0.984)
  Pallas kernels: 123 us -> 121 us
    pallas_call x1, Pallas kernels: 123 us -> 121 us  [per_device(): pl.pallas_call(kernel, name='conv_and_head', out_shape=(jax.ShapeDtypeStr...]
where the time goes in v5:
time: 125 us; the launch traced here: 124 us
  Pallas kernels  121 us (97%)
  local copies, waits for them, and re-layouts  1.97 us (2%)
    pallas_call x1, Pallas kernels, per_device(): pl.pallas_call(kernel, name='conv_and_head', out_shape=(jax.ShapeDtypeStr...  121 us

profile of v5, /device:TPU:1, one launch (start us, length us, event | category | flops | bytes accessed | tf_op | source)
XLA Modules:
  0.0 123.8 jit_solution(11248598995018355250)
XLA Ops:
  0.6 121.2 %conv_and_head.1 = (f32[4,16]{1,0:T(4,128)S(1)}, f32[1024,128]{1,0:T(8,128)S(1)}, f32[16,54]{1,0:T(8,128)S(1)}) custom-call(bf16[16,4,16,128]{3,2,1,0:T(8,128)(2,1)} %bitcast.11, bf16[3456,256]{1,0:T(8,128)(2,1)} %weight_hbm.1, bf16[1024,128]{1,0:T(8,128)(2,1)} %bitcast.12, f32[64,128]{1,0:T(8,128)} %bitcast.13, f32[4,64]{1,0:T(4,128)} %bitcast.14, ...), custom_call_target="tpu_custom_call" | custom-call | tf_op jit(solution)/shard_map/conv_and_head/pallas_call | solution.py:477
  121.8 0.6 copy.12
  122.4 0.8 copy.13
  123.2 0.6 copy.14

commit v6 on v5

--- a/solution.py
+++ b/solution.py
@@ -429,12 +429,6 @@
     turn_copies = group_to(
         "z_lo", OCTET, lambda step: (lo_out.at[(z_lo + step) % 8], lo_in.at[step - 1]), lo_in.at[0:7]
     )
-    feat_copies.wait()
-    lo_slopes.wait()
-    pair = [
-        copy_to("core", 1, feat.at[core], feat.at[core]),
-        copy_to("core", 1, slopes.at[core], slopes.at[core]),
-    ]
     turn_copies.wait()
     total = lo_out[z_lo].astype(F32)
     for step in range(7):
@@ -447,6 +441,12 @@
         lambda step: (hi_out.at[(z_hi + step) % 4], hi_in.at[step - 1]),
         hi_in.at[0:3],
     )
+    feat_copies.wait()
+    lo_slopes.wait()
+    pair = [
+        copy_to("core", 1, feat.at[core], feat.at[core]),
+        copy_to("core", 1, slopes.at[core], slopes.at[core]),
+    ]
     for copy in pair:
         copy.wait()
     over = (((0,), (0,)), ((), ()))

time: 125 us -> 125 us (level)
  no operation moved by 1% of the time
where the time goes in v6:
time: 125 us; the launch traced here: 124 us
  Pallas kernels  121 us (97%)
  local copies, waits for them, and re-layouts  1.97 us (2%)
    pallas_call x1, Pallas kernels, per_device(): pl.pallas_call(kernel, name='conv_and_head', out_shape=(jax.ShapeDtypeStr...  121 us

profile of v6, /device:TPU:1, one launch (start us, length us, event | category | flops | bytes accessed | tf_op | source)
XLA Modules:
  0.0 123.8 jit_solution(4279198933505101867)
XLA Ops:
  0.6 121.2 %conv_and_head.1 = (f32[4,16]{1,0:T(4,128)S(1)}, f32[1024,128]{1,0:T(8,128)S(1)}, f32[16,54]{1,0:T(8,128)S(1)}) custom-call(bf16[16,4,16,128]{3,2,1,0:T(8,128)(2,1)} %bitcast.11, bf16[3456,256]{1,0:T(8,128)(2,1)} %weight_hbm.1, bf16[1024,128]{1,0:T(8,128)(2,1)} %bitcast.12, f32[64,128]{1,0:T(8,128)} %bitcast.13, f32[4,64]{1,0:T(4,128)} %bitcast.14, ...), custom_call_target="tpu_custom_call" | custom-call | tf_op jit(solution)/shard_map/conv_and_head/pallas_call | solution.py:477
  121.8 0.6 copy.12
  122.4 0.8 copy.13
  123.2 0.6 copy.14
